TPU v7x, 256 devices: a whole 4x4x8 slice. The times are simulated.
256 devices in a mesh: flow: 4 (over y_lo, core), gy: 8 (over x, y_hi), gz: 8 (over z).
Axes of the slice: x: 4, y: 4 (y_hi: 2, y_lo: 2; y = y_hi * 2 + y_lo), z: 8, core: 2. Of those that a mesh axis runs over, the one named last changes fastest.
Arguments:
- momentum_sets: float32 [19, 16, 128, 1024], P(None, 'flow', 'gy', 'gz'), may hold values from 0 to 1, as said below
- labels: int32 [16, 128, 1024], P('flow', 'gy', 'gz'), may hold values 0 or 1
- solid_mask: int32 [16, 128, 1024], P('flow', 'gy', 'gz'), may hold values 0 or 1
Outputs:
- momentum_out: float32 [19, 16, 128, 1024], P(None, 'flow', 'gy', 'gz')
- red_out: float32 [7, 16, 128, 1024], P(None, 'flow', 'gy', 'gz')
- blue_out: float32 [7, 16, 128, 1024], P(None, 'flow', 'gy', 'gz')
Inputs may be any that keep to these rules, and one draw needn't show every extreme that they name: `momentum_sets`: every entry is positive.
All inputs are finite; a program needn't handle non-finite values. No bound on the sum of `labels` or of `solid_mask` on one device may be relied on, other than what follows from the above.
Results may differ from a plain program's by a relative error of at most 0.0003.
Values sent between devices are 32-bit elements; how exact they have to be, the bound alone decides.
A program may use at most 64 MiB of HBM per device.

v0:
```python
import functools

import jax
import jax.numpy as jnp
from jax import lax
from jax.experimental import pallas as pl
from jax.experimental.pallas import tpu as pltpu
from jax.sharding import PartitionSpec as P

STEPS = 3
NX, NY, NZ = 4, 16, 128
LO, HI = 8, 8 + NY
ROWS = 32
WETTING = 0.3
TENSION = 0.05
MESH = pl.DeviceIdType.MESH
VMEM_LIMIT = 60 * 1024 * 1024

VELOCITY = (
    (0, 0, 0),
    (1, 0, 0),
    (-1, 0, 0),
    (0, 1, 0),
    (0, -1, 0),
    (0, 0, 1),
    (0, 0, -1),
    (1, 1, 0),
    (-1, -1, 0),
    (1, -1, 0),
    (-1, 1, 0),
    (1, 0, 1),
    (-1, 0, -1),
    (1, 0, -1),
    (-1, 0, 1),
    (0, 1, 1),
    (0, -1, -1),
    (0, 1, -1),
    (0, -1, 1),
)
OPPOSITE = (0, 2, 1, 4, 3, 6, 5, 8, 7, 10, 9, 12, 11, 14, 13, 16, 15, 18, 17)
PAIRS = ((1, 2), (3, 4), (5, 6), (7, 8), (9, 10), (11, 12), (13, 14), (15, 16), (17, 18))

X_UP = [("f", i) for i in (1, 7, 9, 11, 13)] + [("r", 1), ("b", 1)]
X_DOWN = [("f", i) for i in (2, 8, 10, 12, 14)] + [("r", 2), ("b", 2)]
EVERY = [("f", i) for i in range(19)] + [("r", i) for i in range(7)] + [("b", i) for i in range(7)]
ORDER = X_UP + X_DOWN + [name for name in EVERY if name not in X_UP + X_DOWN]
SLOT = {name: place for place, name in enumerate(ORDER)}
Y_FACE = {
    1: (("f", 3), ("r", 3), ("f", 7), ("f", 10), ("f", 15), ("f", 17), ("b", 3)),
    -1: (("f", 4), ("r", 4), ("f", 9), ("f", 8), ("f", 18), ("f", 16), ("b", 4)),
}
Z_FACE = {
    1: (("f", 5), ("f", 11), ("f", 14), ("f", 15), ("f", 18), ("r", 5), ("b", 5)),
    -1: (("f", 6), ("f", 13), ("f", 12), ("f", 17), ("f", 16), ("r", 6), ("b", 6)),
}
Z_MOVING = Z_FACE[1] + Z_FACE[-1]
UNROLLED = {name: place for place, name in enumerate(Z_MOVING)}
DIRECTIONS = VELOCITY[1:]
WAY = {offset: place for place, offset in enumerate(DIRECTIONS)}
SIDE = {1: 0, -1: 1}
YZ_WAY = {(1, 1): 0, (1, -1): 1, (-1, 1): 2, (-1, -1): 3}
OTHERS = sorted(DIRECTIONS[2:], key=lambda offset: (abs(offset[2]), abs(offset[0])))


def kernel(
    momentum_in,
    labels_in,
    solid_in,
    every_out,
    state,
    labels,
    solid,
    scalars,
    scalars_down,
    scalars_up,
    posts,
    unrolled,
    speed,
    colour,
    phase_y,
    phase_z,
    phase_yz,
    phase_y_got,
    phase_edge_got,
    phase_z_got,
    post_y,
    post_z,
    post_yz,
    post_y_got,
    post_edge_got,
    post_z_got,
    in_sem,
    out_sem,
    send_sem,
    recv_sem,
    *,
    sizes,
):
    here = tuple(lax.axis_index(axis) for axis in ("flow", "gy", "gz"))

    def neighbour(offset):
        return tuple(
            here[axis] if offset[axis] == 0 else lax.rem(here[axis] + offset[axis] + sizes[axis], sizes[axis])
            for axis in range(3)
        )

    closed = {
        (1, -1): here[1] == 0,
        (1, 1): here[1] == sizes[1] - 1,
        (2, -1): here[2] == 0,
        (2, 1): here[2] == sizes[2] - 1,
    }
    lane = lax.broadcasted_iota(jnp.int32, (8, NZ), 1)
    row_lane = lax.broadcasted_iota(jnp.int32, (1, NZ), 1)

    loads = [
        pltpu.make_async_copy(solid_in, solid, in_sem.at[0]),
        pltpu.make_async_copy(labels_in, labels, in_sem.at[1]),
        pltpu.make_async_copy(momentum_in, state.at[pl.ds(0, 19)], in_sem.at[2]),
    ]
    for load in loads:
        load.start()

    barrier = pltpu.get_barrier_semaphore()
    for offset in DIRECTIONS:
        pl.semaphore_signal(barrier, inc=1, device_id=neighbour(offset), device_id_type=MESH)

    def remote(source, target, turn, offset):
        way = WAY[offset]
        return pltpu.make_async_remote_copy(
            src_ref=source,
            dst_ref=target,
            send_sem=send_sem.at[turn, way],
            recv_sem=recv_sem.at[turn, way],
            device_id=neighbour(offset),
            device_id_type=MESH,
        )

    def phase_copies(step):
        first, count = (0, 2) if step == 0 else (step + 1, 1)
        copies = []
        for offset in DIRECTIONS:
            dx, dy, dz = offset
            way = WAY[offset]
            if dx != 0 and dy != 0:
                source = phase_y.at[step, SIDE[dy], pl.ds((NX - 1) * count if dx == 1 else 0, count)]
                target = phase_edge_got.at[step, way, pl.ds(0, count)]
            elif dy != 0 and dz != 0:
                source = phase_yz.at[step, YZ_WAY[(dy, dz)]]
                target = phase_edge_got.at[step, way, pl.ds(0, 1)]
            elif dy != 0:
                source = phase_y.at[step, SIDE[dy], pl.ds(0, NX * count)]
                target = phase_y_got.at[step, SIDE[dy], pl.ds(0, NX * count)]
            elif dz != 0:
                source = phase_z.at[step, SIDE[dz]]
                target = phase_z_got.at[step, way]
            else:
                near, far = (NX, 0) if offset[0] == 1 else (1, NX + 1)
                copies.append(
                    remote(
                        scalars.at[pl.ds(first, count), near, pl.ds(LO, NY)],
                        scalars.at[pl.ds(first, count), far, pl.ds(LO, NY)],
                        2 * step,
                        offset,
                    )
                )
                continue
            copies.append(remote(source, target, 2 * step, offset))
        return dict(zip(DIRECTIONS, copies))

    def post_x_copies(step):
        copies = {}
        for sign, first, near, far in ((1, 0, NX, 0), (-1, 7, 1, NX + 1)):
            copies[(sign, 0, 0)] = remote(
                posts.at[step, pl.ds(first, 7), near, pl.ds(LO, NY)],
                posts.at[step, pl.ds(first, 7), far, pl.ds(LO, NY)],
                2 * step + 1,
                (sign, 0, 0),
            )
        return copies

    def post_other_copies(step):
        copies = {}
        for offset in OTHERS:
            dx, dy, dz = offset
            way = WAY[offset]
            if dy != 0 and dx == 0 and dz == 0:
                source, target = post_y.at[step, SIDE[dy]], post_y_got.at[step, SIDE[dy]]
            elif dx != 0 and dy != 0:
                line = Y_FACE[dy].index(("f", VELOCITY.index(offset))) * 4 + (NX - 1 if dx == 1 else 0)
                source, target = post_y.at[step, SIDE[dy], line], post_edge_got.at[step, way]
            elif dy != 0:
                source, target = post_yz.at[step, YZ_WAY[(dy, dz)]], post_edge_got.at[step, way]
            else:
                source, target = post_z.at[step, SIDE[dz]], post_z_got.at[step, way]
            copies[offset] = remote(source, target, 2 * step + 1, offset)
        return copies

    def pack_z(tile, place, sign, packed):
        moved = pltpu.roll(tile, place + 1 if sign == 1 else place, axis=1)
        return jnp.where(lane == place, moved, packed)

    def unpack_z(packed, place, sign):
        return pltpu.roll(packed, (128 - place) % 128 if sign == 1 else 127 - place, axis=1)

    def edge_lane(sign):
        return 0 if sign == 1 else NZ - 1

    def set_phase(step, x, values, packed):
        first, count = (0, 2) if step == 0 else (step + 1, 1)
        up, down = packed
        for entry, value in enumerate(values):
            scalars[first + entry, x + 1, LO:HI, :] = value
            for dy, edge in ((1, HI - 1), (-1, LO)):
                phase_y[step, SIDE[dy], x * count + entry] = scalars[first + entry, x + 1, edge : edge + 1, :]
            for half in range(2):
                tile = value[8 * half : 8 * half + 8]
                place = entry * 8 + 2 * x + half
                up = pack_z(tile, place, 1, up)
                down = pack_z(tile, place, -1, down)
        return up, down

    def send_phase(step, packed):
        for dz in (1, -1):
            phase_z[step, SIDE[dz]] = packed[SIDE[dz]]
            for dy, edge in ((1, 7), (-1, 0)):
                phase_yz[step, YZ_WAY[(dy, dz)], 0] = phase_z[step, SIDE[dz], edge : edge + 1, :]
        copies = phase_copies(step)
        for copy in copies.values():
            copy.start()
        return copies

    def unpack_phase(step, copies):
        first, count = (0, 2) if step == 0 else (step + 1, 1)
        fills = (0.0, WETTING) if step == 0 else (WETTING,)
        shifted = {1: scalars_down, -1: scalars_up}

        def cover(offset, value, fill):
            for axis in (1, 2):
                if offset[axis] != 0:
                    value = jnp.where(closed[(axis, -offset[axis])], fill, value)
            return value

        def arrive(*offsets):
            for offset in offsets:
                copies[offset].wait_recv()

        def shift_plane(entry, plane, dz, face, column):
            for half in range(2):
                rows = slice(LO + 8 * half, LO + 8 * half + 8)
                value = scalars[first + entry, plane, rows, :]
                place = entry * 8 + 2 * column + half
                ghost = cover((0, 0, dz), unpack_z(face, place, dz), fills[entry])
                shifted[dz][min(first + entry, 1), plane, rows, :] = jnp.where(
                    lane == edge_lane(dz), ghost, pltpu.roll(value, 1 if dz == 1 else 127, axis=1)
                )

        for copy in copies.values():
            copy.wait_send()
        for dz in (1, -1):
            arrive((0, 0, dz))
            face = phase_z_got[step, WAY[(0, 0, dz)]]
            for entry in range(count):
                for x in range(NX):
                    shift_plane(entry, x + 1, dz, face, x)
        for dy, ghost in ((1, LO - 1), (-1, HI)):
            half = 1 if dy == 1 else 0
            arrive((0, dy, 0), (0, dy, 1), (0, dy, -1))
            for entry in range(count):
                for x in range(NX):
                    line = cover((0, dy, 0), phase_y_got[step, SIDE[dy], x * count + entry], fills[entry])
                    scalars[first + entry, x + 1, ghost : ghost + 1, :] = line
                    for dz in (1, -1):
                        corner = phase_edge_got[step, WAY[(0, dy, dz)], 0]
                        place = entry * 8 + 2 * x + half
                        corner = cover((0, dy, dz), unpack_z(corner, place, dz), fills[entry])
                        shifted[dz][min(first + entry, 1), x + 1, ghost : ghost + 1, :] = jnp.where(
                            row_lane == edge_lane(dz), corner, pltpu.roll(line, 1 if dz == 1 else 127, axis=1)
                        )
        for dx, plane, column in ((1, 0, NX - 1), (-1, NX + 1, 0)):
            for dy, ghost in ((1, LO - 1), (-1, HI)):
                arrive((dx, dy, 0))
                for entry in range(count):
                    line = phase_edge_got[step, WAY[(dx, dy, 0)], entry]
                    scalars[first + entry, plane, ghost : ghost + 1, :] = cover((0, dy, 0), line, fills[entry])
            arrive((dx, 0, 0))
            for dz in (1, -1):
                arrive((dx, 0, dz))
                for entry in range(count):
                    shift_plane(entry, plane, dz, phase_z_got[step, WAY[(dx, 0, dz)]], column)

    def relax_body(step, x):
        total = state[0, x]
        flux = [0.0, 0.0, 0.0]
        for up, down in PAIRS:
            first, second = state[up, x], state[down, x]
            total = total + (first + second)
            difference = first - second
            for axis in range(3):
                if VELOCITY[up][axis] == 1:
                    flux[axis] = flux[axis] + difference
                elif VELOCITY[up][axis] == -1:
                    flux[axis] = flux[axis] - difference
        inverse = 1.0 / total
        velocity = [part * inverse for part in flux]
        phase = scalars[step + 1, x + 1, LO:HI, :]
        tau = 1.3 - 0.3 * phase
        rate = 1.0 / tau
        keep = 1.0 - rate
        for axis in range(3):
            speed[axis, x] = velocity[axis]
        if step == 0:
            red = total * (0.05 + 0.9 * labels[x].astype(jnp.float32))
            blue = total - red
            colour[0, x] = red
            colour[1, x] = blue
        shifted = [velocity[0] + tau * inverse * 0.001, velocity[1], velocity[2]]
        square = shifted[0] * shifted[0] + shifted[1] * shifted[1] + shifted[2] * shifted[2]
        scale = rate * total
        base = scale * (1.0 - 1.5 * square)
        state[0, x] = keep * state[0, x] + base * (1.0 / 3.0)
        face, edge = base * (1.0 / 18.0), base * (1.0 / 36.0)
        for up, down in PAIRS:
            along = 0.0
            for axis in range(3):
                if VELOCITY[up][axis] == 1:
                    along = along + shifted[axis]
                elif VELOCITY[up][axis] == -1:
                    along = along - shifted[axis]
            push = scale * along
            if up < 7:
                even, odd = face + 0.25 * (push * along), push * (1.0 / 6.0)
            else:
                even, odd = edge + 0.125 * (push * along), push * (1.0 / 12.0)
            state[up, x] = keep * state[up, x] + (even + odd)
            state[down, x] = keep * state[down, x] + (even - odd)

    def gradient_at(step, x):
        def at(buffer, place, plane, dy):
            return buffer[place, plane, LO + dy : HI + dy, :]

        here_ = step + 1

        def spread(plane):
            return (
                2.0 * at(scalars, here_, plane, 0)
                + (at(scalars, here_, plane, 1) + at(scalars, here_, plane, -1))
                + (at(scalars_up, 1, plane, 0) + at(scalars_down, 1, plane, 0))
            )

        def slope_y(plane):
            return at(scalars, here_, plane, 1) - at(scalars, here_, plane, -1)

        def slope_z(plane):
            return at(scalars_up, 1, plane, 0) - at(scalars_down, 1, plane, 0)

        low, mid, high = x, x + 1, x + 2
        up_up, up_down = at(scalars_up, 1, mid, 1), at(scalars_up, 1, mid, -1)
        down_up, down_down = at(scalars_down, 1, mid, 1), at(scalars_down, 1, mid, -1)
        along_x = spread(high) - spread(low)
        along_y = 2.0 * slope_y(mid) + (slope_y(high) + slope_y(low)) + ((up_up - up_down) + (down_up - down_down))
        along_z = 2.0 * slope_z(mid) + (slope_z(high) + slope_z(low)) + ((up_up - down_up) + (up_down - down_down))
        return [part * (1.0 / 12.0) for part in (along_x, along_y, along_z)]

    def put_post(step, x, name, value, packed):
        kind, number = name
        offset = VELOCITY[number]
        if offset[1] != 0:
            sign = offset[1]
            edge = HI - 1 if sign == 1 else LO
        up, down = packed
        if offset[2] != 0:
            unrolled[UNROLLED[name], x] = value
            sign_z = offset[2]
            first = Z_FACE[sign_z].index(name) * 8
            for half in range(2):
                tile = value[8 * half : 8 * half + 8]
                place = first + 2 * x + half
                if sign_z == 1:
                    up = pack_z(tile, place, 1, up)
                else:
                    down = pack_z(tile, place, -1, down)
            value = pltpu.roll(value, 1 if sign_z == 1 else 127, axis=1)
        posts[step, SLOT[name], x + 1, LO:HI, :] = value
        if offset[1] != 0:
            line = Y_FACE[sign].index(name) * 4 + x
            post_y[step, SIDE[sign], line] = posts[step, SLOT[name], x + 1, edge : edge + 1, :]
        return up, down

    def collide_body(step, x, packed):
        gradient = gradient_at(step, x)
        squares = [part * part for part in gradient]
        total = squares[0] + squares[1] + squares[2]
        packed = put_post(step, x, ("f", 0), state[0, x], packed)
        third = total * (1.0 / 3.0)
        for up, down in PAIRS:
            if up < 7:
                surface = (TENSION / 18.0) * (squares[(up - 1) // 2] - third)
            else:
                slope = 0.0
                for axis in range(3):
                    if VELOCITY[up][axis] == 1:
                        slope = slope + gradient[axis]
                    elif VELOCITY[up][axis] == -1:
                        slope = slope - gradient[axis]
                surface = (TENSION / 36.0) * (slope * slope - 2.0 * third)
            packed = put_post(step, x, ("f", up), state[up, x] + surface, packed)
            packed = put_post(step, x, ("f", down), state[down, x] + surface, packed)
        red, blue = colour[0, x], colour[1, x]
        mixing = (0.5 * 0.125) * (red * blue / (red + blue)) * lax.rsqrt(jnp.maximum(total, 0.01))
        packed = put_post(step, x, ("r", 0), 0.25 * red, packed)
        packed = put_post(step, x, ("b", 0), 0.25 * blue, packed)
        for axis in range(3):
            drift = 0.5 * speed[axis, x]
            across = mixing * gradient[axis]
            for kind, amount, turn in (("r", red, 1.0), ("b", blue, -1.0)):
                mean = 0.125 * amount
                lean = amount * drift + turn * across
                packed = put_post(step, x, (kind, 2 * axis + 1), mean + lean, packed)
                packed = put_post(step, x, (kind, 2 * axis + 2), mean - lean, packed)
        return packed

    def unpack_posts(step, copies):
        def arrive(*offsets):
            for offset in offsets:
                copies[offset].wait_recv()

        def put_column(dz, entry, plane, face, column):
            slot = SLOT[Z_FACE[dz][entry]]
            for half in range(2):
                rows = slice(LO + 8 * half, LO + 8 * half + 8)
                place = entry * 8 + 2 * column + half
                posts[step, slot, plane, rows, :] = jnp.where(
                    lane == edge_lane(dz), unpack_z(face, place, dz), posts[step, slot, plane, rows, :]
                )

        for copy in copies.values():
            copy.wait_send()
        for dz in (1, -1):
            arrive((0, 0, dz))
            face = post_z_got[step, WAY[(0, 0, dz)]]
            for entry, name in enumerate(Z_FACE[dz]):
                for x in range(NX):
                    plane = x + 1 - VELOCITY[name[1]][0]
                    if 1 <= plane <= NX:
                        put_column(dz, entry, plane, face, plane - 1)
        for dy, ghost in ((1, LO - 1), (-1, HI)):
            half = 1 if dy == 1 else 0
            arrive((0, dy, 0), (0, dy, 1), (0, dy, -1))
            for entry, name in enumerate(Y_FACE[dy]):
                dx, _, dz = VELOCITY[name[1]]
                for x in range(NX):
                    plane = x + 1 - dx
                    if not 1 <= plane <= NX:
                        continue
                    line = post_y_got[step, SIDE[dy], entry * 4 + plane - 1]
                    if dz != 0:
                        corner = post_edge_got[step, WAY[(0, dy, dz)]]
                        place = Z_FACE[dz].index(name) * 8 + 2 * x + half
                        line = jnp.where(row_lane == edge_lane(dz), unpack_z(corner, place, dz), line)
                    posts[step, SLOT[name], plane, ghost : ghost + 1, :] = line
        for dx, plane, column in ((1, 0, NX - 1), (-1, NX + 1, 0)):
            for dy, ghost in ((1, LO - 1), (-1, HI)):
                offset = (dx, dy, 0)
                arrive(offset)
                slot = SLOT[("f", VELOCITY.index(offset))]
                posts[step, slot, plane, ghost : ghost + 1, :] = post_edge_got[step, WAY[offset]]
            arrive((dx, 0, 0))
            for dz in (1, -1):
                offset = (dx, 0, dz)
                arrive(offset)
                entry = Z_FACE[dz].index(("f", VELOCITY.index(offset)))
                put_column(dz, entry, plane, post_z_got[step, WAY[offset]], column)

    def stream_body(step, x, packed):
        last = step == STEPS - 1
        shifted = {0: scalars, 1: scalars_down, -1: scalars_up}
        fluid = scalars[0, x + 1, LO:HI, :] > 0.0
        opened = [fluid]
        for offset in DIRECTIONS:
            dx, dy, dz = offset
            opened.append(shifted[dz][0, x + 1 - dx, LO - dy : HI - dy, :] > 0.0)

        def pulled(kind, number):
            dx, dy, dz = VELOCITY[number]
            arriving = posts[step, SLOT[(kind, number)], x + 1 - dx, LO - dy : HI - dy, :]
            if number == 0:
                return arriving
            back = (kind, OPPOSITE[number])
            if dz != 0:
                bounced = unrolled[UNROLLED[back], x]
            else:
                bounced = posts[step, SLOT[back], x + 1, LO:HI, :]
            return jnp.where(opened[number], arriving, bounced)

        for number in range(19):
            value = pulled("f", number)
            state[number, x] = jnp.where(fluid, value, 0.0) if last else value
        sums = []
        for place, kind in enumerate(("r", "b")):
            total = 0.0
            for number in range(7):
                value = pulled(kind, number)
                if last:
                    state[19 + 7 * place + number, x] = jnp.where(fluid, value, 0.0)
                else:
                    total = total + value
            if not last:
                colour[place, x] = total
                sums.append(total)
        if last:
            return packed
        red, blue = sums
        phase = jnp.where(fluid, (red - blue) / (red + blue), WETTING)
        return set_phase(step + 1, x, [phase], packed)

    blank = jnp.zeros((8, NZ), jnp.float32)

    def first_phase(x, packed):
        fluid = 1.0 - solid[x].astype(jnp.float32)
        phase = jnp.where(fluid > 0.0, -0.9 + 1.8 * labels[x].astype(jnp.float32), WETTING)
        return set_phase(0, x, [fluid, phase], packed)

    loads[0].wait()
    loads[1].wait()
    packed = lax.fori_loop(0, NX, first_phase, (blank, blank), unroll=True)
    pl.semaphore_wait(barrier, len(DIRECTIONS))
    copies = send_phase(0, packed)
    loads[2].wait()
    for step in range(STEPS):
        lax.fori_loop(0, NX, lambda x, _: relax_body(step, x), None, unroll=True)
        unpack_phase(step, copies)
        packed = (blank, blank)
        packed = lax.fori_loop(0, 2, lambda turn, p: collide_body(step, 3 - 3 * turn, p), packed, unroll=True)
        copies = post_x_copies(step)
        for copy in copies.values():
            copy.start()
        packed = lax.fori_loop(1, 3, lambda x, p: collide_body(step, x, p), packed, unroll=True)
        for dz in (1, -1):
            post_z[step, SIDE[dz]] = packed[SIDE[dz]]
            for dy, edge in ((1, 7), (-1, 0)):
                post_yz[step, YZ_WAY[(dy, dz)]] = post_z[step, SIDE[dz], edge : edge + 1, :]
        others = post_other_copies(step)
        for copy in others.values():
            copy.start()
        unpack_posts(step, {**copies, **others})
        if step < STEPS - 1:
            packed = lax.fori_loop(0, NX, lambda x, p: stream_body(step, x, p), (blank, blank), unroll=True)
            copies = send_phase(step + 1, packed)
        else:
            lax.fori_loop(0, NX, lambda x, p: stream_body(step, x, p), (blank, blank), unroll=True)

    store = pltpu.make_async_copy(state, every_out, out_sem)
    store.start()
    store.wait()


def hand_out(every, momentum_out, red_out, blue_out, sem):
    copies = []
    first = 0
    for place, target in enumerate((momentum_out, red_out, blue_out)):
        count = target.shape[0]
        copies.append(pltpu.make_async_copy(every.at[pl.ds(first, count)], target, sem.at[place]))
        first += count
    for copy in copies:
        copy.start()
    for copy in copies:
        copy.wait()


def shards(sizes, momentum_sets, labels, solid_mask):
    block = (NX, NY, NZ)
    f32 = jnp.float32
    anywhere = pl.BlockSpec(memory_space=pl.ANY)
    vmem = lambda *shape, dtype=f32: pltpu.VMEM(shape, dtype)
    every = pl.pallas_call(
        functools.partial(kernel, sizes=sizes),
        out_shape=jax.ShapeDtypeStruct((33,) + block, f32),
        in_specs=[anywhere] * 3,
        out_specs=anywhere,
        scratch_shapes=[
            vmem(33, *block),
            vmem(*block, dtype=jnp.int32),
            vmem(*block, dtype=jnp.int32),
            vmem(1 + STEPS, NX + 2, ROWS, NZ),
            vmem(2, NX + 2, ROWS, NZ),
            vmem(2, NX + 2, ROWS, NZ),
            vmem(STEPS, 33, NX + 2, ROWS, NZ),
            vmem(14, *block),
            vmem(3, *block),
            vmem(2, *block),
            vmem(STEPS, 2, 8, 1, NZ),
            vmem(STEPS, 2, 8, NZ),
            vmem(STEPS, 4, 1, 1, NZ),
            vmem(STEPS, 2, 8, 1, NZ),
            vmem(STEPS, 18, 2, 1, NZ),
            vmem(STEPS, 18, 8, NZ),
            vmem(STEPS, 2, 28, 1, NZ),
            vmem(STEPS, 2, 8, NZ),
            vmem(STEPS, 4, 1, NZ),
            vmem(STEPS, 2, 28, 1, NZ),
            vmem(STEPS, 18, 1, NZ),
            vmem(STEPS, 18, 8, NZ),
            pltpu.SemaphoreType.DMA((3,)),
            pltpu.SemaphoreType.DMA,
            pltpu.SemaphoreType.DMA((2 * STEPS, 18)),
            pltpu.SemaphoreType.DMA((2 * STEPS, 18)),
        ],
        compiler_params=pltpu.CompilerParams(
            collective_id=0, has_side_effects=True, vmem_limit_bytes=VMEM_LIMIT
        ),
        cost_estimate=pl.CostEstimate(flops=15_000_000, bytes_accessed=1_800_000, transcendentals=0),
    )(momentum_sets, labels, solid_mask)
    return pl.pallas_call(
        hand_out,
        out_shape=[jax.ShapeDtypeStruct((count,) + block, f32) for count in (19, 7, 7)],
        in_specs=[anywhere],
        out_specs=[anywhere] * 3,
        scratch_shapes=[pltpu.SemaphoreType.DMA((3,))],
        compiler_params=pltpu.CompilerParams(vmem_limit_bytes=VMEM_LIMIT),
        cost_estimate=pl.CostEstimate(flops=0, bytes_accessed=2_200_000, transcendentals=0),
    )(every)


def solution(mesh):
    sizes = tuple(mesh.shape[axis] for axis in ("flow", "gy", "gz"))
    split = P("flow", "gy", "gz")
    split_sets = P(None, "flow", "gy", "gz")
    return jax.shard_map(
        functools.partial(shards, sizes),
        mesh=mesh,
        in_specs=(split_sets, split, split),
        out_specs=(split_sets, split_sets, split_sets),
        check_vma=False,
    )
```

profile of v0, /device:TPU:1, one launch (start us, length us, event | category | flops | bytes accessed | tf_op | source)
XLA Modules:
  0.0 85.0 jit_solution(9938277758435650641)
XLA Ops:
  0.6 50.5 %shard_map.58.every = f32[33,4,16,128]{3,2,1,0:T(8,128)} custom-call(f32[19,4,16,128]{3,2,1,0:T(8,128)} %momentum_in.1, s32[4,16,128]{2,1,0:T(8,128)} %labels_in.1, s32[4,16,128]{2,1,0:T(8,128)} %solid_in.1), custom_call_target="tpu_custom_call" | custom-call | flops 15000000 | bytes 1800000 | tf_op jit(solution)/shard_map/pallas_call | solution.py:576
  51.2 33.9 %shard_map.59 = (f32[19,4,16,128]{3,2,1,0:T(8,128)}, f32[7,4,16,128]{3,2,1,0:T(8,128)}, f32[7,4,16,128]{3,2,1,0:T(8,128)}) custom-call(f32[33,4,16,128]{3,2,1,0:T(8,128)} %shard_map.58.every), custom_call_target="tpu_custom_call" | custom-call | bytes 2200000 | tf_op jit(solution)/shard_map/pallas_call | solution.py:614
where the time goes:
time: 85.1 us; the launch traced here: 85 us
  Pallas kernels  84.4 us (99%)
    pallas_call x1, Pallas kernels, shards(): pl.pallas_call(functools.partial(kernel, sizes=sizes), out_shape=jax.Shap...  50.5 us
    pallas_call x1, Pallas kernels, shards(): pl.pallas_call(hand_out, out_shape=[jax.ShapeDtypeStruct((count,) + block...  33.9 us

commit v1 on v0

--- a/solution.py
+++ b/solution.py
@@ -14,7 +14,7 @@
 WETTING = 0.3
 TENSION = 0.05
 MESH = pl.DeviceIdType.MESH
-VMEM_LIMIT = 60 * 1024 * 1024
+VMEM_LIMIT = 40 * 1024 * 1024
 
 VELOCITY = (
     (0, 0, 0),
@@ -59,6 +59,10 @@
 WAY = {offset: place for place, offset in enumerate(DIRECTIONS)}
 SIDE = {1: 0, -1: 1}
 YZ_WAY = {(1, 1): 0, (1, -1): 1, (-1, 1): 2, (-1, -1): 3}
+GROUPS = [
+    [offset for offset in DIRECTIONS if offset[1:] == (dy, dz)]
+    for dy, dz in ((0, 0), (1, 0), (-1, 0), (0, 1), (0, -1), (1, 1), (1, -1), (-1, 1), (-1, -1))
+]
 OTHERS = sorted(DIRECTIONS[2:], key=lambda offset: (abs(offset[2]), abs(offset[0])))
 
 
@@ -66,7 +70,6 @@
     momentum_in,
     labels_in,
     solid_in,
-    every_out,
     state,
     labels,
     solid,
@@ -90,7 +93,6 @@
     post_edge_got,
     post_z_got,
     in_sem,
-    out_sem,
     send_sem,
     recv_sem,
     *,
@@ -110,6 +112,26 @@
         (2, -1): here[2] == 0,
         (2, 1): here[2] == sizes[2] - 1,
     }
+    def has(offset):
+        known = [jnp.logical_not(closed[(axis, offset[axis])]) for axis in (1, 2) if offset[axis] != 0]
+        return functools.reduce(jnp.logical_and, known) if known else None
+
+    def when(condition, action):
+        if condition is None:
+            action()
+        else:
+            pl.when(condition)(action)
+
+    def each(copies, verb, backward=False):
+        for group in GROUPS:
+            mine = [copies[offset] for offset in group if offset in copies]
+            dy, dz = group[0][1:]
+            if mine:
+                when(
+                    has((0, -dy, -dz) if backward else (0, dy, dz)),
+                    lambda mine=mine: [getattr(copy, verb)() for copy in mine] and None,
+                )
+
     lane = lax.broadcasted_iota(jnp.int32, (8, NZ), 1)
     row_lane = lax.broadcasted_iota(jnp.int32, (1, NZ), 1)
 
@@ -122,8 +144,16 @@
         load.start()
 
     barrier = pltpu.get_barrier_semaphore()
-    for offset in DIRECTIONS:
-        pl.semaphore_signal(barrier, inc=1, device_id=neighbour(offset), device_id_type=MESH)
+    for group in GROUPS:
+
+        def greet(group=group):
+            for offset in group:
+                pl.semaphore_signal(barrier, inc=1, device_id=neighbour(offset), device_id_type=MESH)
+
+        when(has((0,) + group[0][1:]), greet)
+    beside_y = 2 - closed[(1, 1)].astype(jnp.int32) - closed[(1, -1)].astype(jnp.int32)
+    beside_z = 2 - closed[(2, 1)].astype(jnp.int32) - closed[(2, -1)].astype(jnp.int32)
+    beside = 2 + 3 * (beside_y + beside_z) + beside_y * beside_z
 
     def remote(source, target, turn, offset):
         way = WAY[offset]
@@ -136,8 +166,8 @@
             device_id_type=MESH,
         )
 
-    def phase_copies(step):
-        first, count = (0, 2) if step == 0 else (step + 1, 1)
+    def phase_copies(step, initial):
+        first, count = (0, 2) if initial else (step + 1, 1)
         copies = []
         for offset in DIRECTIONS:
             dx, dy, dz = offset
@@ -207,7 +237,8 @@
         return 0 if sign == 1 else NZ - 1
 
     def set_phase(step, x, values, packed):
-        first, count = (0, 2) if step == 0 else (step + 1, 1)
+        count = len(values)
+        first = 0 if count == 2 else step + 1
         up, down = packed
         for entry, value in enumerate(values):
             scalars[first + entry, x + 1, LO:HI, :] = value
@@ -220,20 +251,22 @@
                 down = pack_z(tile, place, -1, down)
         return up, down
 
-    def send_phase(step, packed):
+    def send_phase(step, packed, initial):
         for dz in (1, -1):
             phase_z[step, SIDE[dz]] = packed[SIDE[dz]]
             for dy, edge in ((1, 7), (-1, 0)):
                 phase_yz[step, YZ_WAY[(dy, dz)], 0] = phase_z[step, SIDE[dz], edge : edge + 1, :]
-        copies = phase_copies(step)
-        for copy in copies.values():
-            copy.start()
+        copies = phase_copies(step, initial)
+        each(copies, "start")
         return copies
 
-    def unpack_phase(step, copies):
-        first, count = (0, 2) if step == 0 else (step + 1, 1)
-        fills = (0.0, WETTING) if step == 0 else (WETTING,)
+    def unpack_phase(step, copies, initial):
+        first, count = (0, 2) if initial else (step + 1, 1)
+        fills = (0.0, WETTING) if initial else (WETTING,)
         shifted = {1: scalars_down, -1: scalars_up}
+
+        def place_of(entry):
+            return entry if initial else 1
 
         def cover(offset, value, fill):
             for axis in (1, 2):
@@ -242,8 +275,7 @@
             return value
 
         def arrive(*offsets):
-            for offset in offsets:
-                copies[offset].wait_recv()
+            each({offset: copies[offset] for offset in offsets}, "wait_recv", backward=True)
 
         def shift_plane(entry, plane, dz, face, column):
             for half in range(2):
@@ -251,12 +283,11 @@
                 value = scalars[first + entry, plane, rows, :]
                 place = entry * 8 + 2 * column + half
                 ghost = cover((0, 0, dz), unpack_z(face, place, dz), fills[entry])
-                shifted[dz][min(first + entry, 1), plane, rows, :] = jnp.where(
+                shifted[dz][place_of(entry), plane, rows, :] = jnp.where(
                     lane == edge_lane(dz), ghost, pltpu.roll(value, 1 if dz == 1 else 127, axis=1)
                 )
 
-        for copy in copies.values():
-            copy.wait_send()
+        each(copies, "wait_send")
         for dz in (1, -1):
             arrive((0, 0, dz))
             face = phase_z_got[step, WAY[(0, 0, dz)]]
@@ -274,22 +305,20 @@
                         corner = phase_edge_got[step, WAY[(0, dy, dz)], 0]
                         place = entry * 8 + 2 * x + half
                         corner = cover((0, dy, dz), unpack_z(corner, place, dz), fills[entry])
-                        shifted[dz][min(first + entry, 1), x + 1, ghost : ghost + 1, :] = jnp.where(
+                        shifted[dz][place_of(entry), x + 1, ghost : ghost + 1, :] = jnp.where(
                             row_lane == edge_lane(dz), corner, pltpu.roll(line, 1 if dz == 1 else 127, axis=1)
                         )
         for dx, plane, column in ((1, 0, NX - 1), (-1, NX + 1, 0)):
+            arrive((dx, 1, 0), (dx, -1, 0), (dx, 0, 0), (dx, 0, 1), (dx, 0, -1))
             for dy, ghost in ((1, LO - 1), (-1, HI)):
-                arrive((dx, dy, 0))
                 for entry in range(count):
                     line = phase_edge_got[step, WAY[(dx, dy, 0)], entry]
                     scalars[first + entry, plane, ghost : ghost + 1, :] = cover((0, dy, 0), line, fills[entry])
-            arrive((dx, 0, 0))
             for dz in (1, -1):
-                arrive((dx, 0, dz))
                 for entry in range(count):
                     shift_plane(entry, plane, dz, phase_z_got[step, WAY[(dx, 0, dz)]], column)
 
-    def relax_body(step, x):
+    def relax_body(step, x, initial):
         total = state[0, x]
         flux = [0.0, 0.0, 0.0]
         for up, down in PAIRS:
@@ -309,7 +338,7 @@
         keep = 1.0 - rate
         for axis in range(3):
             speed[axis, x] = velocity[axis]
-        if step == 0:
+        if initial:
             red = total * (0.05 + 0.9 * labels[x].astype(jnp.float32))
             blue = total - red
             colour[0, x] = red
@@ -422,8 +451,7 @@
 
     def unpack_posts(step, copies):
         def arrive(*offsets):
-            for offset in offsets:
-                copies[offset].wait_recv()
+            each({offset: copies[offset] for offset in offsets}, "wait_recv", backward=True)
 
         def put_column(dz, entry, plane, face, column):
             slot = SLOT[Z_FACE[dz][entry]]
@@ -434,8 +462,7 @@
                     lane == edge_lane(dz), unpack_z(face, place, dz), posts[step, slot, plane, rows, :]
                 )
 
-        for copy in copies.values():
-            copy.wait_send()
+        each(copies, "wait_send")
         for dz in (1, -1):
             arrive((0, 0, dz))
             face = post_z_got[step, WAY[(0, 0, dz)]]
@@ -460,20 +487,17 @@
                         line = jnp.where(row_lane == edge_lane(dz), unpack_z(corner, place, dz), line)
                     posts[step, SLOT[name], plane, ghost : ghost + 1, :] = line
         for dx, plane, column in ((1, 0, NX - 1), (-1, NX + 1, 0)):
+            arrive((dx, 1, 0), (dx, -1, 0), (dx, 0, 0), (dx, 0, 1), (dx, 0, -1))
             for dy, ghost in ((1, LO - 1), (-1, HI)):
                 offset = (dx, dy, 0)
-                arrive(offset)
                 slot = SLOT[("f", VELOCITY.index(offset))]
                 posts[step, slot, plane, ghost : ghost + 1, :] = post_edge_got[step, WAY[offset]]
-            arrive((dx, 0, 0))
             for dz in (1, -1):
                 offset = (dx, 0, dz)
-                arrive(offset)
                 entry = Z_FACE[dz].index(("f", VELOCITY.index(offset)))
                 put_column(dz, entry, plane, post_z_got[step, WAY[offset]], column)
 
     def stream_body(step, x, packed):
-        last = step == STEPS - 1
         shifted = {0: scalars, 1: scalars_down, -1: scalars_up}
         fluid = scalars[0, x + 1, LO:HI, :] > 0.0
         opened = [fluid]
@@ -494,22 +518,16 @@
             return jnp.where(opened[number], arriving, bounced)
 
         for number in range(19):
-            value = pulled("f", number)
-            state[number, x] = jnp.where(fluid, value, 0.0) if last else value
+            state[number, x] = jnp.where(fluid, pulled("f", number), 0.0)
         sums = []
         for place, kind in enumerate(("r", "b")):
             total = 0.0
             for number in range(7):
                 value = pulled(kind, number)
-                if last:
-                    state[19 + 7 * place + number, x] = jnp.where(fluid, value, 0.0)
-                else:
-                    total = total + value
-            if not last:
-                colour[place, x] = total
-                sums.append(total)
-        if last:
-            return packed
+                state[19 + 7 * place + number, x] = jnp.where(fluid, value, 0.0)
+                total = total + value
+            colour[place, x] = total
+            sums.append(total)
         red, blue = sums
         phase = jnp.where(fluid, (red - blue) / (red + blue), WETTING)
         return set_phase(step + 1, x, [phase], packed)
@@ -524,35 +542,34 @@
     loads[0].wait()
     loads[1].wait()
     packed = lax.fori_loop(0, NX, first_phase, (blank, blank), unroll=True)
-    pl.semaphore_wait(barrier, len(DIRECTIONS))
-    copies = send_phase(0, packed)
+    pl.semaphore_wait(barrier, beside)
+    copies = send_phase(0, packed, True)
     loads[2].wait()
-    for step in range(STEPS):
-        lax.fori_loop(0, NX, lambda x, _: relax_body(step, x), None, unroll=True)
-        unpack_phase(step, copies)
+    lax.fori_loop(0, NX, lambda x, _: relax_body(0, x, True), None, unroll=True)
+    unpack_phase(0, copies, True)
+
+    def step_body(step, _):
         packed = (blank, blank)
         packed = lax.fori_loop(0, 2, lambda turn, p: collide_body(step, 3 - 3 * turn, p), packed, unroll=True)
         copies = post_x_copies(step)
-        for copy in copies.values():
-            copy.start()
+        each(copies, "start")
         packed = lax.fori_loop(1, 3, lambda x, p: collide_body(step, x, p), packed, unroll=True)
         for dz in (1, -1):
             post_z[step, SIDE[dz]] = packed[SIDE[dz]]
             for dy, edge in ((1, 7), (-1, 0)):
                 post_yz[step, YZ_WAY[(dy, dz)]] = post_z[step, SIDE[dz], edge : edge + 1, :]
         others = post_other_copies(step)
-        for copy in others.values():
-            copy.start()
+        each(others, "start")
         unpack_posts(step, {**copies, **others})
-        if step < STEPS - 1:
-            packed = lax.fori_loop(0, NX, lambda x, p: stream_body(step, x, p), (blank, blank), unroll=True)
-            copies = send_phase(step + 1, packed)
-        else:
-            lax.fori_loop(0, NX, lambda x, p: stream_body(step, x, p), (blank, blank), unroll=True)
-
-    store = pltpu.make_async_copy(state, every_out, out_sem)
-    store.start()
-    store.wait()
+        packed = lax.fori_loop(0, NX, lambda x, p: stream_body(step, x, p), (blank, blank), unroll=True)
+
+        @pl.when(step < STEPS - 1)
+        def _():
+            copies = send_phase(step + 1, packed, False)
+            lax.fori_loop(0, NX, lambda x, _: relax_body(step + 1, x, False), None, unroll=True)
+            unpack_phase(step + 1, copies, False)
+
+    lax.fori_loop(0, STEPS, step_body, None)
 
 
 def hand_out(every, momentum_out, red_out, blue_out, sem):
@@ -571,25 +588,23 @@
 def shards(sizes, momentum_sets, labels, solid_mask):
     block = (NX, NY, NZ)
     f32 = jnp.float32
-    anywhere = pl.BlockSpec(memory_space=pl.ANY)
     vmem = lambda *shape, dtype=f32: pltpu.VMEM(shape, dtype)
     every = pl.pallas_call(
         functools.partial(kernel, sizes=sizes),
-        out_shape=jax.ShapeDtypeStruct((33,) + block, f32),
-        in_specs=[anywhere] * 3,
-        out_specs=anywhere,
+        out_shape=vmem(33, *block),
+        in_specs=[pl.BlockSpec(memory_space=pltpu.HBM)] * 3,
+        out_specs=pl.BlockSpec(memory_space=pltpu.VMEM),
         scratch_shapes=[
-            vmem(33, *block),
             vmem(*block, dtype=jnp.int32),
             vmem(*block, dtype=jnp.int32),
-            vmem(1 + STEPS, NX + 2, ROWS, NZ),
+            vmem(2 + STEPS, NX + 2, ROWS, NZ),
             vmem(2, NX + 2, ROWS, NZ),
             vmem(2, NX + 2, ROWS, NZ),
             vmem(STEPS, 33, NX + 2, ROWS, NZ),
             vmem(14, *block),
             vmem(3, *block),
             vmem(2, *block),
-            vmem(STEPS, 2, 8, 1, NZ),
+            vmem(STEPS + 1, 2, 8, 1, NZ),
             vmem(STEPS, 2, 8, NZ),
             vmem(STEPS, 4, 1, 1, NZ),
             vmem(STEPS, 2, 8, 1, NZ),
@@ -602,7 +617,6 @@
             vmem(STEPS, 18, 1, NZ),
             vmem(STEPS, 18, 8, NZ),
             pltpu.SemaphoreType.DMA((3,)),
-            pltpu.SemaphoreType.DMA,
             pltpu.SemaphoreType.DMA((2 * STEPS, 18)),
             pltpu.SemaphoreType.DMA((2 * STEPS, 18)),
         ],
@@ -610,14 +624,13 @@
             collective_id=0, has_side_effects=True, vmem_limit_bytes=VMEM_LIMIT
         ),
         cost_estimate=pl.CostEstimate(flops=15_000_000, bytes_accessed=1_800_000, transcendentals=0),
-    )(momentum_sets, labels, solid_mask)
+    )(*(pltpu.with_memory_space_constraint(array, pltpu.HBM) for array in (momentum_sets, labels, solid_mask)))
     return pl.pallas_call(
         hand_out,
         out_shape=[jax.ShapeDtypeStruct((count,) + block, f32) for count in (19, 7, 7)],
-        in_specs=[anywhere],
-        out_specs=[anywhere] * 3,
+        in_specs=[pl.BlockSpec(memory_space=pltpu.VMEM)],
+        out_specs=[pl.BlockSpec(memory_space=pltpu.HBM)] * 3,
         scratch_shapes=[pltpu.SemaphoreType.DMA((3,))],
-        compiler_params=pltpu.CompilerParams(vmem_limit_bytes=VMEM_LIMIT),
         cost_estimate=pl.CostEstimate(flops=0, bytes_accessed=2_200_000, transcendentals=0),
     )(every)
 

time: 85.1 us -> 46.8 us (0.55)
  Pallas kernels: 84.4 us -> 45 us
  local copies, waits for them, and re-layouts: 0 us -> 0.98 us
    pallas_call x1, Pallas kernels: 33.9 us -> 2.23 us  [shards(): pl.pallas_call(hand_out, out_shape=[jax.ShapeDtypeStruct((count,) + block...]
    pallas_call x1, Pallas kernels: 50.5 us -> 42.8 us  [shards(): pl.pallas_call(functools.partial(kernel, sizes=sizes), out_shape=vmem(33,...]
    unnamed x0 -> x2, local copies, waits for them, and re-layouts: none -> 0.98 us
where the time goes in v1:
time: 46.8 us; the launch traced here: 46.6 us
  Pallas kernels  45 us (96%)
  local copies, waits for them, and re-layouts  0.98 us (2%)
  between operations  0.65 us (1%)
    pallas_call x1, Pallas kernels, shards(): pl.pallas_call(functools.partial(kernel, sizes=sizes), out_shape=vmem(33,...  42.8 us
    pallas_call x1, Pallas kernels, shards(): pl.pallas_call(hand_out, out_shape=[jax.ShapeDtypeStruct((count,) + block...  2.23 us
    unnamed x2, local copies, waits for them, and re-layouts  0.98 us

profile of v1, /device:TPU:1, one launch (start us, length us, event | category | flops | bytes accessed | tf_op | source)
XLA Modules:
  0.0 46.6 jit_solution(14193235093545402337)
XLA Ops:
  0.6 42.8 %shard_map.58.every = f32[33,4,16,128]{3,2,1,0:T(8,128)S(1)} custom-call(f32[19,4,16,128]{3,2,1,0:T(8,128)} %momentum_in.1, s32[4,16,128]{2,1,0:T(8,128)} %labels_in.1, s32[4,16,128]{2,1,0:T(8,128)} %solid_in.1), custom_call_target="tpu_custom_call" | custom-call | flops 15000000 | bytes 1800000 | tf_op jit(solution)/shard_map/pallas_call | solution.py:592
  43.4 0.0 copy-start
  43.4 1.0 %copy-done = f32[33,4,16,128]{3,2,1,0:T(8,128)} copy-done((f32[33,4,16,128]{3,2,1,0:T(8,128)}, f32[33,4,16,128]{3,2,1,0:T(8,128)S(1)}, u32[]{:S(2)}) %copy-start) | copy-done | bytes 1081368
  44.4 2.2 %shard_map.59 = (f32[19,4,16,128]{3,2,1,0:T(8,128)}, f32[7,4,16,128]{3,2,1,0:T(8,128)}, f32[7,4,16,128]{3,2,1,0:T(8,128)}) custom-call(f32[33,4,16,128]{3,2,1,0:T(8,128)} %copy-done), custom_call_target="tpu_custom_call" | custom-call | bytes 2200000 | tf_op jit(solution)/shard_map/pallas_call | solution.py:628
Async XLA Ops:
  43.4 1.0 %copy-start = (f32[33,4,16,128]{3,2,1,0:T(8,128)}, f32[33,4,16,128]{3,2,1,0:T(8,128)S(1)}, u32[]{:S(2)}) copy-start(f32[33,4,16,128]{3,2,1,0:T(8,128)S(1)} %shard_map.58.every) | copy-start | bytes 3244036

commit v2 on v1

v2 whole, which is shorter than its diff:
```python
import functools

import jax
import jax.numpy as jnp
from jax import lax
from jax.experimental import pallas as pl
from jax.experimental.pallas import tpu as pltpu
from jax.sharding import PartitionSpec as P

STEPS = 3
NX, NY, NZ = 4, 16, 128
LO, HI = 8, 8 + NY
ROWS = 32
WETTING = 0.3
TENSION = 0.05
MESH = pl.DeviceIdType.MESH
VMEM_LIMIT = 40 * 1024 * 1024

VELOCITY = (
    (0, 0, 0),
    (1, 0, 0),
    (-1, 0, 0),
    (0, 1, 0),
    (0, -1, 0),
    (0, 0, 1),
    (0, 0, -1),
    (1, 1, 0),
    (-1, -1, 0),
    (1, -1, 0),
    (-1, 1, 0),
    (1, 0, 1),
    (-1, 0, -1),
    (1, 0, -1),
    (-1, 0, 1),
    (0, 1, 1),
    (0, -1, -1),
    (0, 1, -1),
    (0, -1, 1),
)
OPPOSITE = (0, 2, 1, 4, 3, 6, 5, 8, 7, 10, 9, 12, 11, 14, 13, 16, 15, 18, 17)
PAIRS = ((1, 2), (3, 4), (5, 6), (7, 8), (9, 10), (11, 12), (13, 14), (15, 16), (17, 18))

X_UP = [("f", i) for i in (1, 7, 9, 11, 13)] + [("r", 1), ("b", 1)]
X_DOWN = [("f", i) for i in (2, 8, 10, 12, 14)] + [("r", 2), ("b", 2)]
EVERY = [("f", i) for i in range(19)] + [("r", i) for i in range(7)] + [("b", i) for i in range(7)]
ORDER = X_UP + X_DOWN + [name for name in EVERY if name not in X_UP + X_DOWN]
SLOT = {name: place for place, name in enumerate(ORDER)}
Y_FACE = {
    1: (("f", 3), ("r", 3), ("f", 7), ("f", 10), ("f", 15), ("f", 17), ("b", 3)),
    -1: (("f", 4), ("r", 4), ("f", 9), ("f", 8), ("f", 18), ("f", 16), ("b", 4)),
}
Z_FACE = {
    1: (("f", 5), ("f", 11), ("f", 14), ("f", 15), ("f", 18), ("r", 5), ("b", 5)),
    -1: (("f", 6), ("f", 13), ("f", 12), ("f", 17), ("f", 16), ("r", 6), ("b", 6)),
}
Z_MOVING = Z_FACE[1] + Z_FACE[-1]
UNROLLED = {name: place for place, name in enumerate(Z_MOVING)}
DIRECTIONS = VELOCITY[1:]
CORNERS = tuple((a, b, c) for a in (1, -1) for b in (1, -1) for c in (1, -1))
NEIGHBOURS = DIRECTIONS + CORNERS
SIDE = {1: 0, -1: 1}
TURN = {0: 0, 1: 1, -1: 2}
FACE = {(1, 1): 3, (1, -1): 4, (0, 1): 1, (0, -1): 2, (2, 1): 5, (2, -1): 6}
IN_Z, SUM_Z, X_Z, Y_Z = 40, 56, 72, 88
SUM_Y, X_Y, Z_Y, ROWS_Y = 28, 36, 40, 42
Y_XY, SUM_XY, X_XY, ROWS_XY = 1, 3, 5, 7
ROWS_Y_ALL = ROWS_Y + 2 * ROWS_XY
Y_PART, Z_PART, ROWS_PART = 32, 40, 56
CLASSES = ((1, 0), (-1, 0), (1, 1), (1, -1), (-1, 1), (-1, -1), (0, 1), (0, -1))
CLASS = {way: place for place, way in enumerate(CLASSES)}
X_CLASS = {1: 8, -1: 9}
PART_CLASS = {1: 10, -1: 11}
ACROSS_YZ = tuple(("f", number) for number in (15, 16, 17, 18))


def kernel(
    momentum_in,
    labels_in,
    solid_in,
    state,
    labels,
    solid,
    scalars,
    scalars_down,
    scalars_up,
    posts,
    unrolled,
    speed,
    colour,
    phase_y,
    phase_z,
    phase_yz,
    phase_y_got,
    phase_z_got,
    phase_yz_got,
    post_y,
    post_z,
    post_row,
    post_xy,
    post_part,
    post_y_got,
    post_z_got,
    post_row_got,
    post_part_got,
    partial,
    in_sem,
    send_sem,
    recv_sem,
    *,
    sizes,
):
    here = tuple(lax.axis_index(axis) for axis in ("flow", "gy", "gz"))

    flow = {
        0: here[0],
        1: jnp.where(here[0] == sizes[0] - 1, 0, here[0] + 1),
        -1: jnp.where(here[0] == 0, sizes[0] - 1, here[0] - 1),
    }
    lateral = [{0: here[axis], 1: here[axis] + 1, -1: here[axis] - 1} for axis in (1, 2)]

    def neighbour(offset):
        return (flow[offset[0]], lateral[0][offset[1]], lateral[1][offset[2]])

    closed = {
        (1, -1): here[1] == 0,
        (1, 1): here[1] == sizes[1] - 1,
        (2, -1): here[2] == 0,
        (2, 1): here[2] == sizes[2] - 1,
    }
    def has(offset):
        known = [jnp.logical_not(closed[(axis, offset[axis])]) for axis in (1, 2) if offset[axis] != 0]
        return functools.reduce(jnp.logical_and, known) if known else None

    def when(condition, action):
        if condition is None:
            action()
        else:
            pl.when(condition)(action)

    def by_class(action, backward=False):
        for dy, dz in CLASSES:
            when(has((0, -dy, -dz) if backward else (0, dy, dz)), functools.partial(action, dy, dz))

    lane = lax.broadcasted_iota(jnp.int32, (8, NZ), 1)
    wide_lane = lax.broadcasted_iota(jnp.int32, (NY, NZ), 1)
    wide_row = lax.broadcasted_iota(jnp.int32, (NY, NZ), 0)
    row = lax.broadcasted_iota(jnp.int32, (8, NZ), 0)
    row_lane = lax.broadcasted_iota(jnp.int32, (1, NZ), 1)

    loads = [
        pltpu.make_async_copy(solid_in, solid, in_sem.at[0]),
        pltpu.make_async_copy(labels_in, labels, in_sem.at[1]),
        pltpu.make_async_copy(momentum_in, state.at[pl.ds(0, 19)], in_sem.at[2]),
    ]
    for load in loads:
        load.start()

    def send(source, target, turn, place, offset):
        pltpu.make_async_remote_copy(
            src_ref=source,
            dst_ref=target,
            send_sem=send_sem.at[turn, place],
            recv_sem=recv_sem.at[turn, place],
            device_id=neighbour(offset),
            device_id_type=MESH,
        ).start()

    def await_bytes(sems, turn, place, like):
        pltpu.make_async_copy(like, like, sems.at[turn, place]).wait()

    def send_phase_class(dy, dz):
        place = CLASS[(dy, dz)]
        if dz == 0:
            side = SIDE[dy]
            send(phase_y.at[side], phase_y_got.at[side, pl.ds(0, 8)], 0, place, (0, dy, 0))
            for dx, line, target in ((1, 6, 8), (-1, 0, 10)):
                source = phase_y.at[side, pl.ds(line, 2)]
                send(source, phase_y_got.at[side, pl.ds(target, 2)], 0, place, (dx, dy, 0))
        elif dy == 0:
            side = SIDE[dz]
            for dx in (0, 1, -1):
                send(phase_z.at[side], phase_z_got.at[side, TURN[dx]], 0, place, (dx, 0, dz))
        else:
            sides = SIDE[dy], SIDE[dz]
            send(phase_yz.at[sides], phase_yz_got.at[sides], 0, place, (0, dy, dz))

    def phase_like(dy, dz):
        if dz == 0:
            return phase_y_got.at[SIDE[dy]]
        if dy == 0:
            return phase_z_got.at[SIDE[dz]]
        return phase_yz_got.at[SIDE[dy], SIDE[dz]]

    def phase_plane(plane):
        return scalars.at[pl.ds(0, 2), plane, pl.ds(LO, NY)]

    def post_plane(step, dx, plane):
        return posts.at[step, pl.ds(0 if dx == 1 else 7, 7), plane, pl.ds(LO, NY)]

    def send_post_class(step, fused, dy, dz):
        turn, place = step + 1, CLASS[(dy, dz)]
        if dz == 0:
            side = SIDE[dy]
            send(post_y.at[step, side], post_y_got.at[step, side, pl.ds(0, ROWS_Y)], turn, place, (0, dy, 0))
            for dx in (1, -1):
                target = post_y_got.at[step, side, pl.ds(ROWS_Y + ROWS_XY * SIDE[dx], ROWS_XY)]
                send(post_xy.at[step, SIDE[dx], side], target, turn, place, (dx, dy, 0))
        elif dy == 0:
            side = SIDE[dz]
            for dx in (0, 1, -1):
                send(post_z.at[step, side], post_z_got.at[step, side, TURN[dx]], turn, place, (dx, 0, dz))
        else:
            sides = SIDE[dy], SIDE[dz]
            for dx in (0, 1, -1) if fused else (0,):
                target = post_row_got.at[step, sides[0], sides[1], TURN[dx]]
                send(post_row.at[step, sides[0], sides[1]], target, turn, place, (dx, dy, dz))

    def post_like(step, fused, dy, dz):
        if dz == 0:
            return post_y_got.at[step, SIDE[dy]]
        if dy == 0:
            return post_z_got.at[step, SIDE[dz]]
        return post_row_got.at[step, SIDE[dy], SIDE[dz], pl.ds(0, 3 if fused else 1)]

    def pack_z(tile, place, sign, packed):
        moved = pltpu.roll(tile, place + 1 if sign == 1 else place, axis=1)
        return jnp.where(lane == place, moved, packed)

    def unpack_z(packed, place, sign):
        return pltpu.roll(packed, (128 - place) % 128 if sign == 1 else 127 - place, axis=1)

    def edge_lane(sign):
        return 0 if sign == 1 else NZ - 1

    def set_phase(x, values, packed):
        up, down = packed
        for entry, value in enumerate(values):
            scalars[entry, x + 1, LO:HI, :] = value
            for dy, edge in ((1, HI - 1), (-1, LO)):
                phase_y[SIDE[dy], x * 2 + entry] = scalars[entry, x + 1, edge : edge + 1, :]
            for half in range(2):
                tile = value[8 * half : 8 * half + 8]
                place = entry * 8 + 2 * x + half
                up = pack_z(tile, place, 1, up)
                down = pack_z(tile, place, -1, down)
        return up, down

    def send_phase(packed):
        for dz in (1, -1):
            phase_z[SIDE[dz]] = packed[SIDE[dz]]
            for dy, edge in ((1, 7), (-1, 0)):
                phase_yz[SIDE[dy], SIDE[dz]] = phase_z[SIDE[dz], edge : edge + 1, :]
        by_class(send_phase_class)
        for dx, near, far in ((1, NX, 0), (-1, 1, NX + 1)):
            send(phase_plane(near), phase_plane(far), 0, X_CLASS[dx], (dx, 0, 0))

    def unpack_phase():
        first, count = 0, 2
        fills = (0.0, WETTING)
        shifted = {1: scalars_down, -1: scalars_up}

        def place_of(entry):
            return entry

        def cover(offset, value, fill):
            for axis in (1, 2):
                if offset[axis] != 0:
                    value = jnp.where(closed[(axis, -offset[axis])], fill, value)
            return value

        def arrive(sems, backward):
            by_class(lambda dy, dz: await_bytes(sems, 0, CLASS[(dy, dz)], phase_like(dy, dz)), backward)
            for dx in (1, -1):
                await_bytes(sems, 0, X_CLASS[dx], phase_plane(0))

        def shift_plane(entry, plane, dz, face, column):
            for half in range(2):
                rows = slice(LO + 8 * half, LO + 8 * half + 8)
                value = scalars[first + entry, plane, rows, :]
                place = entry * 8 + 2 * column + half
                ghost = cover((0, 0, dz), unpack_z(face, place, dz), fills[entry])
                shifted[dz][place_of(entry), plane, rows, :] = jnp.where(
                    lane == edge_lane(dz), ghost, pltpu.roll(value, 1 if dz == 1 else 127, axis=1)
                )

        arrive(send_sem, False)
        arrive(recv_sem, True)
        for dz in (1, -1):
            face = phase_z_got[SIDE[dz], 0]
            for entry in range(count):
                for x in range(NX):
                    shift_plane(entry, x + 1, dz, face, x)
        for dy, ghost in ((1, LO - 1), (-1, HI)):
            half = 1 if dy == 1 else 0
            for entry in range(count):
                for x in range(NX):
                    line = cover((0, dy, 0), phase_y_got[SIDE[dy], x * count + entry], fills[entry])
                    scalars[first + entry, x + 1, ghost : ghost + 1, :] = line
                    for dz in (1, -1):
                        corner = phase_yz_got[SIDE[dy], SIDE[dz]]
                        place = entry * 8 + 2 * x + half
                        corner = cover((0, dy, dz), unpack_z(corner, place, dz), fills[entry])
                        shifted[dz][place_of(entry), x + 1, ghost : ghost + 1, :] = jnp.where(
                            row_lane == edge_lane(dz), corner, pltpu.roll(line, 1 if dz == 1 else 127, axis=1)
                        )
        for dx, plane, column in ((1, 0, NX - 1), (-1, NX + 1, 0)):
            for dy, ghost in ((1, LO - 1), (-1, HI)):
                for entry in range(count):
                    line = phase_y_got[SIDE[dy], 8 + 2 * SIDE[dx] + entry]
                    scalars[first + entry, plane, ghost : ghost + 1, :] = cover((0, dy, 0), line, fills[entry])
            for dz in (1, -1):
                for entry in range(count):
                    shift_plane(entry, plane, dz, phase_z_got[SIDE[dz], TURN[dx]], column)

    def relax_body(step, x, initial):
        total = state[0, x]
        flux = [0.0, 0.0, 0.0]
        for up, down in PAIRS:
            first, second = state[up, x], state[down, x]
            total = total + (first + second)
            difference = first - second
            for axis in range(3):
                if VELOCITY[up][axis] == 1:
                    flux[axis] = flux[axis] + difference
                elif VELOCITY[up][axis] == -1:
                    flux[axis] = flux[axis] - difference
        inverse = 1.0 / total
        velocity = [part * inverse for part in flux]
        phase = scalars[step + 1, x + 1, LO:HI, :]
        tau = 1.3 - 0.3 * phase
        rate = 1.0 / tau
        keep = 1.0 - rate
        for axis in range(3):
            speed[axis, x] = velocity[axis]
        if initial:
            red = total * (0.05 + 0.9 * labels[x].astype(jnp.float32))
            blue = total - red
            colour[0, x] = red
            colour[1, x] = blue
        shifted = [velocity[0] + tau * inverse * 0.001, velocity[1], velocity[2]]
        square = shifted[0] * shifted[0] + shifted[1] * shifted[1] + shifted[2] * shifted[2]
        scale = rate * total
        base = scale * (1.0 - 1.5 * square)
        state[0, x] = keep * state[0, x] + base * (1.0 / 3.0)
        face, edge = base * (1.0 / 18.0), base * (1.0 / 36.0)
        for up, down in PAIRS:
            along = 0.0
            for axis in range(3):
                if VELOCITY[up][axis] == 1:
                    along = along + shifted[axis]
                elif VELOCITY[up][axis] == -1:
                    along = along - shifted[axis]
            push = scale * along
            if up < 7:
                even, odd = face + 0.25 * (push * along), push * (1.0 / 6.0)
            else:
                even, odd = edge + 0.125 * (push * along), push * (1.0 / 12.0)
            state[up, x] = keep * state[up, x] + (even + odd)
            state[down, x] = keep * state[down, x] + (even - odd)

    def gradient_at(step, x):
        def at(buffer, place, plane, dy):
            return buffer[place, plane, LO + dy : HI + dy, :]

        here_ = step + 1

        def spread(plane):
            return (
                2.0 * at(scalars, here_, plane, 0)
                + (at(scalars, here_, plane, 1) + at(scalars, here_, plane, -1))
                + (at(scalars_up, 1, plane, 0) + at(scalars_down, 1, plane, 0))
            )

        def slope_y(plane):
            return at(scalars, here_, plane, 1) - at(scalars, here_, plane, -1)

        def slope_z(plane):
            return at(scalars_up, 1, plane, 0) - at(scalars_down, 1, plane, 0)

        low, mid, high = x, x + 1, x + 2
        up_up, up_down = at(scalars_up, 1, mid, 1), at(scalars_up, 1, mid, -1)
        down_up, down_down = at(scalars_down, 1, mid, 1), at(scalars_down, 1, mid, -1)
        along_x = spread(high) - spread(low)
        along_y = 2.0 * slope_y(mid) + (slope_y(high) + slope_y(low)) + ((up_up - up_down) + (down_up - down_down))
        along_z = 2.0 * slope_z(mid) + (slope_z(high) + slope_z(low)) + ((up_up - down_up) + (up_down - down_down))
        return [part * (1.0 / 12.0) for part in (along_x, along_y, along_z)]

    def put_post(step, x, name, value, packed, fluid=None):
        kind, number = name
        offset = VELOCITY[number]
        value = jnp.where(fluid, value, 0.0)
        if offset[1] != 0:
            sign = offset[1]
            edge = HI - 1 if sign == 1 else LO
        up, down = packed
        if offset[2] != 0:
            unrolled[UNROLLED[name], x] = value
            sign_z = offset[2]
            first = Z_FACE[sign_z].index(name) * 8
            for half in range(2):
                tile = value[8 * half : 8 * half + 8]
                place = first + 2 * x + half
                if sign_z == 1:
                    up = pack_z(tile, place, 1, up)
                else:
                    down = pack_z(tile, place, -1, down)
            value = pltpu.roll(value, 1 if sign_z == 1 else 127, axis=1)
            if name not in ACROSS_YZ:
                value = jnp.where(wide_lane == edge_lane(sign_z), 0.0, value)
        posts[step, SLOT[name], x + 1, LO:HI, :] = value
        if offset[1] != 0:
            line = Y_FACE[sign].index(name) * 4 + x
            post_y[step, SIDE[sign], line] = posts[step, SLOT[name], x + 1, edge : edge + 1, :]
        return up, down

    def collide_body(step, x, packed):
        gradient = gradient_at(step, x)
        squares = [part * part for part in gradient]
        total = squares[0] + squares[1] + squares[2]
        fluid = scalars[0, x + 1, LO:HI, :] > 0.0
        packed = put_post(step, x, ("f", 0), state[0, x], packed, fluid)
        third = total * (1.0 / 3.0)
        for up, down in PAIRS:
            if up < 7:
                surface = (TENSION / 18.0) * (squares[(up - 1) // 2] - third)
            else:
                slope = 0.0
                for axis in range(3):
                    if VELOCITY[up][axis] == 1:
                        slope = slope + gradient[axis]
                    elif VELOCITY[up][axis] == -1:
                        slope = slope - gradient[axis]
                surface = (TENSION / 36.0) * (slope * slope - 2.0 * third)
            packed = put_post(step, x, ("f", up), state[up, x] + surface, packed, fluid)
            packed = put_post(step, x, ("f", down), state[down, x] + surface, packed, fluid)
        red, blue = colour[0, x], colour[1, x]
        mixing = (0.5 * 0.125) * (red * blue / (red + blue)) * lax.rsqrt(jnp.maximum(total, 0.01))
        packed = put_post(step, x, ("r", 0), 0.25 * red, packed, fluid)
        packed = put_post(step, x, ("b", 0), 0.25 * blue, packed, fluid)
        for axis in range(3):
            drift = 0.5 * speed[axis, x]
            across = mixing * gradient[axis]
            for kind, amount, turn in (("r", red, 1.0), ("b", blue, -1.0)):
                mean = 0.125 * amount
                lean = amount * drift + turn * across
                packed = put_post(step, x, (kind, 2 * axis + 1), mean + lean, packed, fluid)
                packed = put_post(step, x, (kind, 2 * axis + 2), mean - lean, packed, fluid)
        return packed

    def state_at(name):
        return {"f": 0, "r": 19, "b": 26}[name[0]] + name[1]

    def opened_at(x, offset):
        dx, dy, dz = offset
        return shifted_scalars[dz][0, x + 1 - dx, LO - dy : HI - dy, :] > 0.0

    def bounced_at(step, x, name):
        back = (name[0], OPPOSITE[name[1]])
        if VELOCITY[name[1]][2] != 0:
            return unrolled[UNROLLED[back], x]
        return posts[step, SLOT[back], x + 1, LO:HI, :]

    def stream_inside(step, x, end, last):
        fluid = scalars[0, x + 1, LO:HI, :] > 0.0
        names = [name for name in EVERY if (last or name[0] == "f") and name not in ACROSS_YZ]
        for name in names:
            dx, dy, dz = VELOCITY[name[1]]
            if name[1] == 0:
                value = posts[step, SLOT[name], x + 1, LO:HI, :]
            else:
                if dx != 0 and dx == end:
                    arriving = 0.0
                else:
                    arriving = posts[step, SLOT[name], x + 1 - dx, LO - dy : HI - dy, :]
                value = jnp.where(opened_at(x, (dx, dy, dz)), arriving, bounced_at(step, x, name))
            state[state_at(name), x] = jnp.where(fluid, value, 0.0) if last else value

    def stream_across(step, x, last):
        fluid = scalars[0, x + 1, LO:HI, :] > 0.0
        for name in ACROSS_YZ:
            dx, dy, dz = VELOCITY[name[1]]
            arriving = posts[step, SLOT[name], x + 1, LO - dy : HI - dy, :]
            value = jnp.where(opened_at(x, (dx, dy, dz)), arriving, bounced_at(step, x, name))
            state[state_at(name), x] = jnp.where(fluid, value, 0.0) if last else value

    def add_arrived(step, last):
        def wanted(name):
            return last or name[0] == "f"

        def kept(x, rows, value):
            if not last:
                return value
            return jnp.where(scalars[0, x + 1, LO + rows.start : LO + rows.stop, :] > 0.0, value, 0.0)

        def z_columns(name, dx, column, half):
            dz = VELOCITY[name[1]][2]
            place = Z_FACE[dz].index(name) * 8 + 2 * column + half
            face = post_z_got[step, SIDE[dz], TURN[dx]]
            return jnp.where(lane == edge_lane(dz), unpack_z(face, place, dz), 0.0)

        for dx, end, ghost, column, names in ((1, 0, 0, NX - 1, X_UP), (-1, NX - 1, NX + 1, 0, X_DOWN)):
            for name in names:
                if not wanted(name):
                    continue
                _, dy, dz = VELOCITY[name[1]]
                if dy != 0:
                    row_ghost = LO - 1 if dy == 1 else HI
                    line = post_y_got[step, SIDE[dy], ROWS_Y + ROWS_XY * SIDE[dx]]
                    posts[step, SLOT[name], ghost, row_ghost : row_ghost + 1, :] = line
                for half in range(2):
                    rows = slice(8 * half, 8 * half + 8)
                    first = LO + 8 * half - dy
                    value = posts[step, SLOT[name], ghost, first : first + 8, :]
                    if dz != 0:
                        value = value + z_columns(name, dx, column, half)
                    state[state_at(name), end, rows, :] = state[state_at(name), end, rows, :] + kept(end, rows, value)
        for dz in (1, -1):
            for name in Z_FACE[dz]:
                if name in ACROSS_YZ or not wanted(name):
                    continue
                for x in range(NX):
                    source = x - VELOCITY[name[1]][0]
                    if not 0 <= source < NX:
                        continue
                    for half in range(2):
                        rows = slice(8 * half, 8 * half + 8)
                        value = kept(x, rows, z_columns(name, 0, source, half))
                        state[state_at(name), x, rows, :] = state[state_at(name), x, rows, :] + value
        for dy, edge in ((1, 0), (-1, NY - 1)):
            rows = slice(edge, edge + 1)
            for entry, name in enumerate(Y_FACE[dy]):
                if name in ACROSS_YZ or not wanted(name):
                    continue
                for x in range(NX):
                    source = x - VELOCITY[name[1]][0]
                    if not 0 <= source < NX:
                        continue
                    value = kept(x, rows, post_y_got[step, SIDE[dy], entry * 4 + source])
                    state[state_at(name), x, rows, :] = state[state_at(name), x, rows, :] + value
        for name in ACROSS_YZ:
            _, dy, dz = VELOCITY[name[1]]
            entry, entry_z = Y_FACE[dy].index(name), Z_FACE[dz].index(name)
            half_y = 1 if dy == 1 else 0
            ghost = LO - 1 if dy == 1 else HI
            for x in range(NX):
                for half in range(2):
                    rows = slice(LO + 8 * half, LO + 8 * half + 8)
                    place = entry_z * 8 + 2 * x + half
                    face = post_z_got[step, SIDE[dz], 0]
                    posts[step, SLOT[name], x + 1, rows, :] = jnp.where(
                        lane == edge_lane(dz), unpack_z(face, place, dz), posts[step, SLOT[name], x + 1, rows, :]
                    )
                corner = unpack_z(post_row_got[step, SIDE[dy], SIDE[dz], 0], entry_z * 8 + 2 * x + half_y, dz)
                line = jnp.where(row_lane == edge_lane(dz), corner, post_y_got[step, SIDE[dy], entry * 4 + x])
                posts[step, SLOT[name], x + 1, ghost : ghost + 1, :] = line

    shifted_scalars = {0: scalars, 1: scalars_down, -1: scalars_up}

    def add_up(step, packed):
        up, down = packed
        for x in range(NX):
            for place, kind in enumerate(("r", "b")):
                total = posts[step, SLOT[(kind, 0)], x + 1, LO:HI, :]
                for number in range(1, 7):
                    dx, dy, dz = VELOCITY[number]
                    plane = x + 1 - dx
                    opened = shifted_scalars[dz][0, plane, LO - dy : HI - dy, :] > 0.0
                    back = (kind, OPPOSITE[number])
                    if dz != 0:
                        bounced = unrolled[UNROLLED[back], x]
                    else:
                        bounced = posts[step, SLOT[back], x + 1, LO:HI, :]
                    if 1 <= plane <= NX:
                        arriving = posts[step, SLOT[(kind, number)], plane, LO - dy : HI - dy, :]
                    else:
                        arriving = 0.0
                    total = total + jnp.where(opened, arriving, bounced)
                partial[place, x] = total
                for half in range(2):
                    tile = total[8 * half : 8 * half + 8]
                    lanes = SUM_Z + 8 * place + 2 * x + half
                    up, down = pack_z(tile, lanes, 1, up), pack_z(tile, lanes, -1, down)
                for dx, end in ((1, NX - 1), (-1, 0)):
                    if x == end:
                        post_part[step, SIDE[dx], NY * place : NY * place + NY, :] = total
                for dy, edge in ((1, NY - 1), (-1, 0)):
                    post_y[step, SIDE[dy], SUM_Y + 4 * place + x] = partial[place, x, edge : edge + 1, :]
                for dy, half in ((1, 1), (-1, 0)):
                    rows = slice(LO + 8 * half, LO + 8 * half + 8)
                    tile = posts[step, SLOT[(kind, FACE[(1, dy)])], x + 1, rows, :]
                    lanes = Y_Z + 8 * place + 2 * x + (0 if dy == 1 else 1)
                    up, down = pack_z(tile, lanes, 1, up), pack_z(tile, lanes, -1, down)
        for place, kind in enumerate(("r", "b")):
            for dx, end in ((1, NX - 1), (-1, 0)):
                slot = SLOT[(kind, FACE[(0, dx)])]
                for half in range(2):
                    tile = posts[step, slot, end + 1, LO + 8 * half : LO + 8 * half + 8, :]
                    lanes = X_Z + 8 * place + (0 if dx == 1 else 6) + half
                    up, down = pack_z(tile, lanes, 1, up), pack_z(tile, lanes, -1, down)
                for dy, edge in ((1, HI - 1), (-1, LO)):
                    line = posts[step, slot, end + 1, edge : edge + 1, :]
                    post_y[step, SIDE[dy], X_Y + 2 * SIDE[dx] + place] = line
                    post_xy[step, SIDE[dx], SIDE[dy], X_XY + place] = line
                    post_xy[step, SIDE[dx], SIDE[dy], SUM_XY + place] = partial[place, end, edge - LO : edge - LO + 1, :]
                    line = posts[step, SLOT[(kind, FACE[(1, dy)])], end + 1, edge : edge + 1, :]
                    post_xy[step, SIDE[dx], SIDE[dy], Y_XY + place] = line
                    part = Y_PART + 2 * SIDE[dy] + place
                    post_part[step, SIDE[dx], part : part + 1, :] = line
        return up, down

    def put_edges(step, packed, fused):
        for dx, end in ((1, NX - 1), (-1, 0)):
            for dy, edge in ((1, HI - 1), (-1, LO)):
                slot = SLOT[("f", VELOCITY.index((dx, dy, 0)))]
                post_xy[step, SIDE[dx], SIDE[dy], 0] = posts[step, slot, end + 1, edge : edge + 1, :]
            if fused:
                post_part[step, SIDE[dx], Z_PART : Z_PART + 8, :] = packed[0]
                post_part[step, SIDE[dx], Z_PART + 8 : Z_PART + 16, :] = packed[1]
        for dz in (1, -1):
            post_z[step, SIDE[dz]] = packed[SIDE[dz]]
            for dy, edge in ((1, 7), (-1, 0)):
                line = post_z[step, SIDE[dz], edge : edge + 1, :]
                post_row[step, SIDE[dy], SIDE[dz]] = line
                if fused:
                    post_y[step, SIDE[dy], Z_Y + SIDE[dz]] = line

    def turned(value, lanes):
        return pltpu.roll(value, 128 - lanes, axis=1)

    def ratio(red, blue):
        return (red - blue) / (red + blue)

    def packed_ratio(sums):
        blue = turned(sums, 8)
        return ratio(sums, blue)

    def finish_phase(step):
        here_ = step + 2

        def put(target, entry, plane, rows, value):
            fluid = shifted_scalars[target][0, plane, rows, :] > 0.0
            shifted_scalars[target][entry, plane, rows, :] = jnp.where(fluid, value, WETTING)

        interior = slice(LO, HI)
        z_got = {(dx, dz): post_z_got[step, SIDE[dz], TURN[dx]] for dx in (-1, 0, 1) for dz in (1, -1)}
        row_got = {
            (dx, dy, dz): post_row_got[step, SIDE[dy], SIDE[dz], TURN[dx]]
            for dx in (-1, 0, 1)
            for dy in (1, -1)
            for dz in (1, -1)
        }

        def xy_got(dx, dy, line):
            return post_y_got[step, SIDE[dy], ROWS_Y + ROWS_XY * SIDE[dx] + line]

        def with_columns(value, place, column, dx):
            halves = []
            for half in range(2):
                tile = value[8 * half : 8 * half + 8]
                for dz in (1, -1):
                    lanes = IN_Z + 8 * place + 2 * column + half
                    tile = tile + jnp.where(lane == edge_lane(dz), unpack_z(z_got[(dx, dz)], lanes, dz), 0.0)
                halves.append(tile)
            return jnp.concatenate(halves, axis=0)

        def with_rows(value, rows):
            for dy, edge in ((1, 0), (-1, NY - 1)):
                value = value + jnp.where(wide_row == edge, rows[dy], 0.0)
            return value

        def with_ends(line, offset, place, x):
            dx, dy = offset
            half = 1 if dy == 1 else 0
            for dz in (1, -1):
                lanes = IN_Z + 8 * place + 2 * x + half
                line = line + jnp.where(row_lane == edge_lane(dz), unpack_z(row_got[(dx, dy, dz)], lanes, dz), 0.0)
            return line

        for x in range(NX):
            sums = []
            for place, kind in enumerate(("r", "b")):
                total = partial[place, x]
                for dx, end, ghost in ((1, 0, 0), (-1, NX - 1, NX + 1)):
                    if x == end:
                        total = total + posts[step, SLOT[(kind, FACE[(0, dx)])], ghost, interior, :]
                rows = {}
                for dy in (1, -1):
                    entry = Y_FACE[dy].index((kind, FACE[(1, dy)]))
                    rows[dy] = post_y_got[step, SIDE[dy], entry * 4 + x]
                total = with_columns(with_rows(total, rows), place, x, 0)
                colour[place, x] = total
                sums.append(total)
            put(0, here_, x + 1, interior, ratio(*sums))
        for dx, ghost, end, column in ((1, 0, 0, NX - 1), (-1, NX + 1, NX - 1, 0)):
            sums = []
            lines = {1: [], -1: []}
            for place, kind in enumerate(("r", "b")):
                total = post_part_got[step, SIDE[dx], NY * place : NY * place + NY, :]
                total = total + posts[step, SLOT[(kind, FACE[(0, -dx)])], end + 1, interior, :]
                rows = {dy: xy_got(dx, dy, Y_XY + place) for dy in (1, -1)}
                sums.append(with_columns(with_rows(total, rows), place, column, dx))
                for dy in (1, -1):
                    part = Y_PART + 2 * SIDE[-dy] + place
                    line = (
                        xy_got(dx, dy, SUM_XY + place)
                        + post_part_got[step, SIDE[dx], part : part + 1, :]
                        + post_y_got[step, SIDE[dy], X_Y + 2 * SIDE[-dx] + place]
                    )
                    lines[dy].append(with_ends(line, (dx, dy), place, column))
            put(0, here_, ghost, interior, ratio(*sums))
            for dy, row_ghost in ((1, LO - 1), (-1, HI)):
                put(0, here_, ghost, slice(row_ghost, row_ghost + 1), ratio(*lines[dy]))
        for dy, row_ghost, edge in ((1, LO - 1, LO), (-1, HI, HI - 1)):
            for x in range(NX):
                sums = []
                for place, kind in enumerate(("r", "b")):
                    line = post_y_got[step, SIDE[dy], SUM_Y + 4 * place + x]
                    line = line + posts[step, SLOT[(kind, FACE[(1, -dy)])], x + 1, edge : edge + 1, :]
                    for dx, end in ((1, 0), (-1, NX - 1)):
                        if x == end:
                            line = line + xy_got(dx, dy, X_XY + place)
                    sums.append(with_ends(line, (0, dy), place, x))
                put(0, here_, x + 1, slice(row_ghost, row_ghost + 1), ratio(*sums))
        low_x, high_x = lane % 8 < 2, lane % 8 >= 6
        first_y, last_y = (row == 0) & (lane % 2 == 0), (row == 7) & (lane % 2 == 1)
        row_low_x, row_high_x = row_lane % 8 < 2, row_lane % 8 >= 6
        for dz in (1, -1):

            def with_y(sums, dx):
                sums = sums + jnp.where(first_y, turned(row_got[(dx, 1, dz)], Y_Z), 0.0)
                return sums + jnp.where(last_y, turned(row_got[(dx, -1, dz)], Y_Z), 0.0)

            sums = turned(z_got[(0, dz)], SUM_Z) + turned(post_z[step, SIDE[-dz]], IN_Z)
            sums = sums + jnp.where(low_x, turned(z_got[(1, dz)], X_Z), 0.0)
            sums = sums + jnp.where(high_x, turned(z_got[(-1, dz)], X_Z), 0.0)
            faces = {0: packed_ratio(with_y(sums, 0))}
            for dx in (1, -1):
                part = Z_PART + 8 * SIDE[-dz]
                sums = turned(z_got[(dx, dz)], SUM_Z) + turned(z_got[(0, dz)], X_Z)
                sums = sums + turned(post_part_got[step, SIDE[dx], part : part + 8, :], IN_Z)
                faces[dx] = packed_ratio(with_y(sums, dx))
            for plane in range(NX + 2):
                dx, column = {0: (1, NX - 1), NX + 1: (-1, 0)}.get(plane, (0, plane - 1))
                for half in range(2):
                    rows = slice(LO + 8 * half, LO + 8 * half + 8)
                    value = scalars[here_, plane, rows, :]
                    ghost = unpack_z(faces[dx], 2 * column + half, dz)
                    value = jnp.where(lane == edge_lane(dz), ghost, pltpu.roll(value, 1 if dz == 1 else 127, axis=1))
                    put(dz, 1, plane, rows, value)
            for dy, row_ghost in ((1, LO - 1), (-1, HI)):
                half = 1 if dy == 1 else 0
                edge = 0 if dy == 1 else 7
                sums = turned(row_got[(0, dy, dz)], SUM_Z)
                sums = sums + turned(post_y_got[step, SIDE[dy], Z_Y + SIDE[-dz]], IN_Z)
                sums = sums + turned(post_z_got[step, SIDE[dz], 0, edge : edge + 1, :], Y_Z)
                sums = sums + jnp.where(row_low_x, turned(row_got[(1, dy, dz)], X_Z), 0.0)
                sums = sums + jnp.where(row_high_x, turned(row_got[(-1, dy, dz)], X_Z), 0.0)
                corner = packed_ratio(sums)
                for x in range(NX):
                    line = scalars[here_, x + 1, row_ghost : row_ghost + 1, :]
                    line = pltpu.roll(line, 1 if dz == 1 else 127, axis=1)
                    line = jnp.where(row_lane == edge_lane(dz), unpack_z(corner, 2 * x + half, dz), line)
                    put(dz, 1, x + 1, slice(row_ghost, row_ghost + 1), line)

    blank = jnp.zeros((8, NZ), jnp.float32)

    def first_phase(x, packed):
        fluid = 1.0 - solid[x].astype(jnp.float32)
        phase = jnp.where(fluid > 0.0, -0.9 + 1.8 * labels[x].astype(jnp.float32), WETTING)
        return set_phase(x, [fluid, phase], packed)

    for step in range(STEPS):
        for side in range(2):
            post_y_got[step, side] = jnp.zeros((ROWS_Y_ALL, 1, NZ), jnp.float32)
            for other in range(2):
                post_row_got[step, side, other] = jnp.zeros((3, 1, NZ), jnp.float32)
            for turn in range(3):
                post_z_got[step, side, turn] = blank

    barrier = pltpu.get_barrier_semaphore()

    def greet(dy, dz):
        for dx in (0, 1, -1):
            pl.semaphore_signal(barrier, inc=1, device_id=neighbour((dx, dy, dz)), device_id_type=MESH)

    by_class(greet)
    for dx in (1, -1):
        pl.semaphore_signal(barrier, inc=1, device_id=neighbour((dx, 0, 0)), device_id_type=MESH)
    beside_y = 2 - closed[(1, 1)].astype(jnp.int32) - closed[(1, -1)].astype(jnp.int32)
    beside_z = 2 - closed[(2, 1)].astype(jnp.int32) - closed[(2, -1)].astype(jnp.int32)
    beside = 2 + 3 * (beside_y + beside_z) + 3 * beside_y * beside_z

    for step in range(STEPS):
        for side in range(2):
            post_part[step, side, Y_PART : Y_PART + 8, :] = blank
            if step == STEPS - 1:
                post_y[step, side, SUM_Y:ROWS_Y] = jnp.zeros((ROWS_Y - SUM_Y, 1, NZ), jnp.float32)
                for other in range(2):
                    post_xy[step, side, other, Y_XY:ROWS_XY] = jnp.zeros((ROWS_XY - Y_XY, 1, NZ), jnp.float32)
        for name in Y_FACE[1] + Y_FACE[-1]:
            if name not in ACROSS_YZ:
                ghost = LO - 1 if VELOCITY[name[1]][1] == 1 else HI
                for plane in range(1, NX + 1):
                    posts[step, SLOT[name], plane, ghost : ghost + 1, :] = blank[0:1]

    loads[0].wait()
    loads[1].wait()
    packed = lax.fori_loop(0, NX, first_phase, (blank, blank), unroll=True)
    pl.semaphore_wait(barrier, beside)
    send_phase(packed)
    loads[2].wait()
    lax.fori_loop(0, NX, lambda x, _: relax_body(0, x, True), None, unroll=True)
    unpack_phase()

    def move(step, fused):
        packed = (blank, blank)
        packed = lax.fori_loop(0, 2, lambda turn, p: collide_body(step, 3 - 3 * turn, p), packed, unroll=True)
        for dx, near, far in ((1, NX, 0), (-1, 1, NX + 1)):
            send(post_plane(step, dx, near), post_plane(step, dx, far), step + 1, X_CLASS[dx], (dx, 0, 0))
        packed = lax.fori_loop(1, 3, lambda x, p: collide_body(step, x, p), packed, unroll=True)
        if fused:
            packed = add_up(step, packed)
        put_edges(step, packed, fused)
        by_class(functools.partial(send_post_class, step, fused))
        if fused:
            for dx in (1, -1):
                side = SIDE[dx]
                send(post_part.at[step, side], post_part_got.at[step, side], step + 1, PART_CLASS[dx], (dx, 0, 0))
        last = not fused
        stream_inside(step, 0, 1, last)
        lax.fori_loop(1, NX - 1, lambda x, _: stream_inside(step, x, 0, last), None, unroll=True)
        stream_inside(step, NX - 1, -1, last)

        for sems, backward in ((send_sem, False), (recv_sem, True)):
            by_class(
                lambda dy, dz, sems=sems: await_bytes(
                    sems, step + 1, CLASS[(dy, dz)], post_like(step, fused, dy, dz)
                ),
                backward,
            )
            for dx in (1, -1):
                await_bytes(sems, step + 1, X_CLASS[dx], post_plane(step, dx, 0 if dx == 1 else NX + 1))
                if fused:
                    await_bytes(sems, step + 1, PART_CLASS[dx], post_part_got.at[step, SIDE[dx]])
        if fused:
            finish_phase(step)
        add_arrived(step, last)
        lax.fori_loop(0, NX, lambda x, _: stream_across(step, x, last), None, unroll=True)

    def step_body(step, _):
        move(step, True)
        lax.fori_loop(0, NX, lambda x, _: relax_body(step + 1, x, False), None, unroll=True)

    lax.fori_loop(0, STEPS - 1, step_body, None)
    move(STEPS - 1, False)


def hand_out(every, momentum_out, red_out, blue_out, sem):
    copies = []
    first = 0
    for place, target in enumerate((momentum_out, red_out, blue_out)):
        count = target.shape[0]
        copies.append(pltpu.make_async_copy(every.at[pl.ds(first, count)], target, sem.at[place]))
        first += count
    for copy in copies:
        copy.start()
    for copy in copies:
        copy.wait()


def shards(sizes, momentum_sets, labels, solid_mask):
    block = (NX, NY, NZ)
    f32 = jnp.float32
    vmem = lambda *shape, dtype=f32: pltpu.VMEM(shape, dtype)
    every = pl.pallas_call(
        functools.partial(kernel, sizes=sizes),
        out_shape=vmem(33, *block),
        in_specs=[pl.BlockSpec(memory_space=pltpu.HBM)] * 3,
        out_specs=pl.BlockSpec(memory_space=pltpu.VMEM),
        scratch_shapes=[
            vmem(*block, dtype=jnp.int32),
            vmem(*block, dtype=jnp.int32),
            vmem(1 + STEPS, NX + 2, ROWS, NZ),
            vmem(2, NX + 2, ROWS, NZ),
            vmem(2, NX + 2, ROWS, NZ),
            vmem(STEPS, 33, NX + 2, ROWS, NZ),
            vmem(14, *block),
            vmem(3, *block),
            vmem(2, *block),
            vmem(2, 8, 1, NZ),
            vmem(2, 8, NZ),
            vmem(2, 2, 1, NZ),
            vmem(2, 12, 1, NZ),
            vmem(2, 3, 8, NZ),
            vmem(2, 2, 1, NZ),
            vmem(STEPS, 2, ROWS_Y, 1, NZ),
            vmem(STEPS, 2, 8, NZ),
            vmem(STEPS, 2, 2, 1, NZ),
            vmem(STEPS, 2, 2, ROWS_XY, 1, NZ),
            vmem(STEPS, 2, ROWS_PART, NZ),
            vmem(STEPS, 2, ROWS_Y_ALL, 1, NZ),
            vmem(STEPS, 2, 3, 8, NZ),
            vmem(STEPS, 2, 2, 3, 1, NZ),
            vmem(STEPS, 2, ROWS_PART, NZ),
            vmem(2, *block),
            pltpu.SemaphoreType.DMA((3,)),
            pltpu.SemaphoreType.DMA((1 + STEPS, 12)),
            pltpu.SemaphoreType.DMA((1 + STEPS, 12)),
        ],
        compiler_params=pltpu.CompilerParams(
            collective_id=0, has_side_effects=True, vmem_limit_bytes=VMEM_LIMIT
        ),
        cost_estimate=pl.CostEstimate(flops=15_000_000, bytes_accessed=1_800_000, transcendentals=0),
    )(*(pltpu.with_memory_space_constraint(array, pltpu.HBM) for array in (momentum_sets, labels, solid_mask)))
    return pl.pallas_call(
        hand_out,
        out_shape=[jax.ShapeDtypeStruct((count,) + block, f32) for count in (19, 7, 7)],
        in_specs=[pl.BlockSpec(memory_space=pltpu.VMEM)],
        out_specs=[pl.BlockSpec(memory_space=pltpu.HBM)] * 3,
        scratch_shapes=[pltpu.SemaphoreType.DMA((3,))],
        cost_estimate=pl.CostEstimate(flops=0, bytes_accessed=2_200_000, transcendentals=0),
    )(pltpu.with_memory_space_constraint(every, pltpu.VMEM))


def solution(mesh):
    sizes = tuple(mesh.shape[axis] for axis in ("flow", "gy", "gz"))
    split = P("flow", "gy", "gz")
    split_sets = P(None, "flow", "gy", "gz")
    return jax.shard_map(
        functools.partial(shards, sizes),
        mesh=mesh,
        in_specs=(split_sets, split, split),
        out_specs=(split_sets, split_sets, split_sets),
        check_vma=False,
    )
```

time: 46.8 us -> 35.3 us (0.75)
  Pallas kernels: 45 us -> 34.6 us
  local copies, waits for them, and re-layouts: 0.98 us -> 0 us
    pallas_call x1, Pallas kernels: 42.8 us -> 33.6 us  [shards(): pl.pallas_call(functools.partial(kernel, sizes=sizes), out_shape=vmem(33,...]
    pallas_call x1, Pallas kernels: 2.23 us -> 1 us  [shards(): pl.pallas_call(hand_out, out_shape=[jax.ShapeDtypeStruct((count,) + block...]
    unnamed x2 -> x0, local copies, waits for them, and re-layouts: 0.98 us -> none
where the time goes in v2:
time: 35.3 us; the launch traced here: 35.2 us
  Pallas kernels  34.6 us (98%)
  between operations  0.64 us (2%)
    pallas_call x1, Pallas kernels, shards(): pl.pallas_call(functools.partial(kernel, sizes=sizes), out_shape=vmem(33,...  33.6 us
    pallas_call x1, Pallas kernels, shards(): pl.pallas_call(hand_out, out_shape=[jax.ShapeDtypeStruct((count,) + block...  1 us

profile of v2, /device:TPU:1, one launch (start us, length us, event | category | flops | bytes accessed | tf_op | source)
XLA Modules:
  0.0 35.2 jit_solution(3000252549490565933)
XLA Ops:
  0.6 33.6 %shard_map.58.every = f32[33,4,16,128]{3,2,1,0:T(8,128)S(1)} custom-call(f32[19,4,16,128]{3,2,1,0:T(8,128)} %momentum_in.1, s32[4,16,128]{2,1,0:T(8,128)} %labels_in.1, s32[4,16,128]{2,1,0:T(8,128)} %solid_in.1), custom_call_target="tpu_custom_call" | custom-call | flops 15000000 | bytes 1800000 | tf_op jit(solution)/shard_map/pallas_call | solution.py:875
  34.2 1.0 %shard_map.59 = (f32[19,4,16,128]{3,2,1,0:T(8,128)}, f32[7,4,16,128]{3,2,1,0:T(8,128)}, f32[7,4,16,128]{3,2,1,0:T(8,128)}) custom-call(f32[33,4,16,128]{3,2,1,0:T(8,128)S(1)} %shard_map.58.every), custom_call_target="tpu_custom_call" | custom-call | bytes 2200000 | tf_op jit(solution)/shard_map/pallas_call | solution.py:915

commit v3 on v2

--- a/solution.py
+++ b/solution.py
@@ -66,10 +66,13 @@
 Y_XY, SUM_XY, X_XY, ROWS_XY = 1, 3, 5, 7
 ROWS_Y_ALL = ROWS_Y + 2 * ROWS_XY
 Y_PART, Z_PART, ROWS_PART = 32, 40, 56
-CLASSES = ((1, 0), (-1, 0), (1, 1), (1, -1), (-1, 1), (-1, -1), (0, 1), (0, -1))
+ON_Y, ON_Z = ((1, 0), (-1, 0)), ((0, 1), (0, -1))
+ON_YZ = ((1, 1), (1, -1), (-1, 1), (-1, -1))
+CLASSES = ON_Y + ON_Z + ON_YZ
 CLASS = {way: place for place, way in enumerate(CLASSES)}
 X_CLASS = {1: 8, -1: 9}
 PART_CLASS = {1: 10, -1: 11}
+CORNER_CLASS = {way: 12 + place for place, way in enumerate(ON_YZ)}
 ACROSS_YZ = tuple(("f", number) for number in (15, 16, 17, 18))
 
 
@@ -137,8 +140,8 @@
         else:
             pl.when(condition)(action)
 
-    def by_class(action, backward=False):
-        for dy, dz in CLASSES:
+    def by_class(action, backward=False, classes=CLASSES):
+        for dy, dz in classes:
             when(has((0, -dy, -dz) if backward else (0, dy, dz)), functools.partial(action, dy, dz))
 
     lane = lax.broadcasted_iota(jnp.int32, (8, NZ), 1)
@@ -197,7 +200,7 @@
     def post_plane(step, dx, plane):
         return posts.at[step, pl.ds(0 if dx == 1 else 7, 7), plane, pl.ds(LO, NY)]
 
-    def send_post_class(step, fused, dy, dz):
+    def send_post_class(step, dy, dz):
         turn, place = step + 1, CLASS[(dy, dz)]
         if dz == 0:
             side = SIDE[dy]
@@ -211,16 +214,42 @@
                 send(post_z.at[step, side], post_z_got.at[step, side, TURN[dx]], turn, place, (dx, 0, dz))
         else:
             sides = SIDE[dy], SIDE[dz]
-            for dx in (0, 1, -1) if fused else (0,):
-                target = post_row_got.at[step, sides[0], sides[1], TURN[dx]]
-                send(post_row.at[step, sides[0], sides[1]], target, turn, place, (dx, dy, dz))
-
-    def post_like(step, fused, dy, dz):
+            target = post_row_got.at[step, sides[0], sides[1], pl.ds(0, 1)]
+            send(post_row.at[step, sides[0], sides[1]], target, turn, place, (0, dy, dz))
+
+    def send_corner_class(step, dy, dz):
+        sides = SIDE[dy], SIDE[dz]
+        for dx in (1, -1):
+            target = post_row_got.at[step, sides[0], sides[1], pl.ds(TURN[dx], 1)]
+            send(post_row.at[step, sides[0], sides[1]], target, step + 1, CORNER_CLASS[(dy, dz)], (dx, dy, dz))
+
+    def post_like(step, dy, dz):
         if dz == 0:
             return post_y_got.at[step, SIDE[dy]]
         if dy == 0:
             return post_z_got.at[step, SIDE[dz]]
-        return post_row_got.at[step, SIDE[dy], SIDE[dz], pl.ds(0, 3 if fused else 1)]
+        return post_row_got.at[step, SIDE[dy], SIDE[dz], pl.ds(0, 1)]
+
+    def corner_like(step, dy, dz):
+        return post_row_got.at[step, SIDE[dy], SIDE[dz], pl.ds(1, 2)]
+
+    def await_posts(sems, step, classes, backward):
+        by_class(
+            lambda dy, dz: await_bytes(sems, step + 1, CLASS[(dy, dz)], post_like(step, dy, dz)), backward, classes
+        )
+
+    def await_corners(sems, step, backward):
+        by_class(
+            lambda dy, dz: await_bytes(sems, step + 1, CORNER_CLASS[(dy, dz)], corner_like(step, dy, dz)),
+            backward,
+            ON_YZ,
+        )
+
+    def await_x(sems, step, fused):
+        for dx in (1, -1):
+            await_bytes(sems, step + 1, X_CLASS[dx], post_plane(step, dx, 0 if dx == 1 else NX + 1))
+            if fused:
+                await_bytes(sems, step + 1, PART_CLASS[dx], post_part_got.at[step, SIDE[dx]])
 
     def pack_z(tile, place, sign, packed):
         moved = pltpu.roll(tile, place + 1 if sign == 1 else place, axis=1)
@@ -483,7 +512,7 @@
             value = jnp.where(opened_at(x, (dx, dy, dz)), arriving, bounced_at(step, x, name))
             state[state_at(name), x] = jnp.where(fluid, value, 0.0) if last else value
 
-    def add_arrived(step, last):
+    def arrivals(step, last):
         def wanted(name):
             return last or name[0] == "f"
 
@@ -498,61 +527,71 @@
             face = post_z_got[step, SIDE[dz], TURN[dx]]
             return jnp.where(lane == edge_lane(dz), unpack_z(face, place, dz), 0.0)
 
-        for dx, end, ghost, column, names in ((1, 0, 0, NX - 1, X_UP), (-1, NX - 1, NX + 1, 0, X_DOWN)):
-            for name in names:
-                if not wanted(name):
-                    continue
-                _, dy, dz = VELOCITY[name[1]]
-                if dy != 0:
-                    row_ghost = LO - 1 if dy == 1 else HI
-                    line = post_y_got[step, SIDE[dy], ROWS_Y + ROWS_XY * SIDE[dx]]
-                    posts[step, SLOT[name], ghost, row_ghost : row_ghost + 1, :] = line
-                for half in range(2):
-                    rows = slice(8 * half, 8 * half + 8)
-                    first = LO + 8 * half - dy
-                    value = posts[step, SLOT[name], ghost, first : first + 8, :]
-                    if dz != 0:
-                        value = value + z_columns(name, dx, column, half)
-                    state[state_at(name), end, rows, :] = state[state_at(name), end, rows, :] + kept(end, rows, value)
-        for dz in (1, -1):
-            for name in Z_FACE[dz]:
-                if name in ACROSS_YZ or not wanted(name):
-                    continue
+        def add_z():
+            for dz in (1, -1):
+                for name in Z_FACE[dz]:
+                    if name in ACROSS_YZ or not wanted(name):
+                        continue
+                    for x in range(NX):
+                        source = x - VELOCITY[name[1]][0]
+                        if not 0 <= source < NX:
+                            continue
+                        for half in range(2):
+                            rows = slice(8 * half, 8 * half + 8)
+                            value = kept(x, rows, z_columns(name, 0, source, half))
+                            state[state_at(name), x, rows, :] = state[state_at(name), x, rows, :] + value
+            for name in ACROSS_YZ:
+                dz = VELOCITY[name[1]][2]
+                face = post_z_got[step, SIDE[dz], 0]
                 for x in range(NX):
-                    source = x - VELOCITY[name[1]][0]
-                    if not 0 <= source < NX:
+                    for half in range(2):
+                        rows = slice(LO + 8 * half, LO + 8 * half + 8)
+                        place = Z_FACE[dz].index(name) * 8 + 2 * x + half
+                        posts[step, SLOT[name], x + 1, rows, :] = jnp.where(
+                            lane == edge_lane(dz), unpack_z(face, place, dz), posts[step, SLOT[name], x + 1, rows, :]
+                        )
+
+        def add_xy():
+            for dx, end, ghost, column, names in ((1, 0, 0, NX - 1, X_UP), (-1, NX - 1, NX + 1, 0, X_DOWN)):
+                for name in names:
+                    if not wanted(name):
                         continue
+                    _, dy, dz = VELOCITY[name[1]]
+                    if dy != 0:
+                        row_ghost = LO - 1 if dy == 1 else HI
+                        line = post_y_got[step, SIDE[dy], ROWS_Y + ROWS_XY * SIDE[dx]]
+                        posts[step, SLOT[name], ghost, row_ghost : row_ghost + 1, :] = line
                     for half in range(2):
                         rows = slice(8 * half, 8 * half + 8)
-                        value = kept(x, rows, z_columns(name, 0, source, half))
+                        first = LO + 8 * half - dy
+                        value = posts[step, SLOT[name], ghost, first : first + 8, :]
+                        if dz != 0:
+                            value = value + z_columns(name, dx, column, half)
+                        state[state_at(name), end, rows, :] = state[state_at(name), end, rows, :] + kept(end, rows, value)
+            for dy, edge in ((1, 0), (-1, NY - 1)):
+                rows = slice(edge, edge + 1)
+                for entry, name in enumerate(Y_FACE[dy]):
+                    if name in ACROSS_YZ or not wanted(name):
+                        continue
+                    for x in range(NX):
+                        source = x - VELOCITY[name[1]][0]
+                        if not 0 <= source < NX:
+                            continue
+                        value = kept(x, rows, post_y_got[step, SIDE[dy], entry * 4 + source])
                         state[state_at(name), x, rows, :] = state[state_at(name), x, rows, :] + value
-        for dy, edge in ((1, 0), (-1, NY - 1)):
-            rows = slice(edge, edge + 1)
-            for entry, name in enumerate(Y_FACE[dy]):
-                if name in ACROSS_YZ or not wanted(name):
-                    continue
+
+        def add_across():
+            for name in ACROSS_YZ:
+                _, dy, dz = VELOCITY[name[1]]
+                entry, entry_z = Y_FACE[dy].index(name), Z_FACE[dz].index(name)
+                half = 1 if dy == 1 else 0
+                ghost = LO - 1 if dy == 1 else HI
                 for x in range(NX):
-                    source = x - VELOCITY[name[1]][0]
-                    if not 0 <= source < NX:
-                        continue
-                    value = kept(x, rows, post_y_got[step, SIDE[dy], entry * 4 + source])
-                    state[state_at(name), x, rows, :] = state[state_at(name), x, rows, :] + value
-        for name in ACROSS_YZ:
-            _, dy, dz = VELOCITY[name[1]]
-            entry, entry_z = Y_FACE[dy].index(name), Z_FACE[dz].index(name)
-            half_y = 1 if dy == 1 else 0
-            ghost = LO - 1 if dy == 1 else HI
-            for x in range(NX):
-                for half in range(2):
-                    rows = slice(LO + 8 * half, LO + 8 * half + 8)
-                    place = entry_z * 8 + 2 * x + half
-                    face = post_z_got[step, SIDE[dz], 0]
-                    posts[step, SLOT[name], x + 1, rows, :] = jnp.where(
-                        lane == edge_lane(dz), unpack_z(face, place, dz), posts[step, SLOT[name], x + 1, rows, :]
-                    )
-                corner = unpack_z(post_row_got[step, SIDE[dy], SIDE[dz], 0], entry_z * 8 + 2 * x + half_y, dz)
-                line = jnp.where(row_lane == edge_lane(dz), corner, post_y_got[step, SIDE[dy], entry * 4 + x])
-                posts[step, SLOT[name], x + 1, ghost : ghost + 1, :] = line
+                    corner = unpack_z(post_row_got[step, SIDE[dy], SIDE[dz], 0], entry_z * 8 + 2 * x + half, dz)
+                    line = jnp.where(row_lane == edge_lane(dz), corner, post_y_got[step, SIDE[dy], entry * 4 + x])
+                    posts[step, SLOT[name], x + 1, ghost : ghost + 1, :] = line
+
+        return add_z, add_xy, add_across
 
     shifted_scalars = {0: scalars, 1: scalars_down, -1: scalars_up}
 
@@ -620,7 +659,7 @@
             post_z[step, SIDE[dz]] = packed[SIDE[dz]]
             for dy, edge in ((1, 7), (-1, 0)):
                 line = post_z[step, SIDE[dz], edge : edge + 1, :]
-                post_row[step, SIDE[dy], SIDE[dz]] = line
+                post_row[step, SIDE[dy], SIDE[dz], 0] = line
                 if fused:
                     post_y[step, SIDE[dy], Z_Y + SIDE[dz]] = line
 
@@ -634,7 +673,7 @@
         blue = turned(sums, 8)
         return ratio(sums, blue)
 
-    def finish_phase(step):
+    def finish_phase(step, inside):
         here_ = step + 2
 
         def put(target, entry, plane, rows, value):
@@ -645,7 +684,7 @@
         z_got = {(dx, dz): post_z_got[step, SIDE[dz], TURN[dx]] for dx in (-1, 0, 1) for dz in (1, -1)}
         row_got = {
             (dx, dy, dz): post_row_got[step, SIDE[dy], SIDE[dz], TURN[dx]]
-            for dx in (-1, 0, 1)
+            for dx in (() if inside else (-1, 0, 1))
             for dy in (1, -1)
             for dz in (1, -1)
         }
@@ -676,7 +715,7 @@
                 line = line + jnp.where(row_lane == edge_lane(dz), unpack_z(row_got[(dx, dy, dz)], lanes, dz), 0.0)
             return line
 
-        for x in range(NX):
+        for x in range(NX) if inside else ():
             sums = []
             for place, kind in enumerate(("r", "b")):
                 total = partial[place, x]
@@ -691,6 +730,8 @@
                 colour[place, x] = total
                 sums.append(total)
             put(0, here_, x + 1, interior, ratio(*sums))
+        if inside:
+            return
         for dx, ghost, end, column in ((1, 0, 0, NX - 1), (-1, NX + 1, NX - 1, 0)):
             sums = []
             lines = {1: [], -1: []}
@@ -769,14 +810,6 @@
         phase = jnp.where(fluid > 0.0, -0.9 + 1.8 * labels[x].astype(jnp.float32), WETTING)
         return set_phase(x, [fluid, phase], packed)
 
-    for step in range(STEPS):
-        for side in range(2):
-            post_y_got[step, side] = jnp.zeros((ROWS_Y_ALL, 1, NZ), jnp.float32)
-            for other in range(2):
-                post_row_got[step, side, other] = jnp.zeros((3, 1, NZ), jnp.float32)
-            for turn in range(3):
-                post_z_got[step, side, turn] = blank
-
     barrier = pltpu.get_barrier_semaphore()
 
     def greet(dy, dz):
@@ -789,6 +822,18 @@
     beside_y = 2 - closed[(1, 1)].astype(jnp.int32) - closed[(1, -1)].astype(jnp.int32)
     beside_z = 2 - closed[(2, 1)].astype(jnp.int32) - closed[(2, -1)].astype(jnp.int32)
     beside = 2 + 3 * (beside_y + beside_z) + 3 * beside_y * beside_z
+
+    def clear(dy, dz):
+        for step in range(STEPS):
+            if dz == 0:
+                post_y_got[step, SIDE[dy]] = jnp.zeros((ROWS_Y_ALL, 1, NZ), jnp.float32)
+            elif dy == 0:
+                post_z_got[step, SIDE[dz]] = jnp.zeros((3, 8, NZ), jnp.float32)
+            else:
+                post_row_got[step, SIDE[dy], SIDE[dz]] = jnp.zeros((3, 1, NZ), jnp.float32)
+
+    for dy, dz in CLASSES:
+        pl.when(jnp.logical_not(has((0, -dy, -dz))))(functools.partial(clear, dy, dz))
 
     for step in range(STEPS):
         for side in range(2):
@@ -821,35 +866,38 @@
         if fused:
             packed = add_up(step, packed)
         put_edges(step, packed, fused)
-        by_class(functools.partial(send_post_class, step, fused))
+        by_class(functools.partial(send_post_class, step))
         if fused:
             for dx in (1, -1):
                 side = SIDE[dx]
                 send(post_part.at[step, side], post_part_got.at[step, side], step + 1, PART_CLASS[dx], (dx, 0, 0))
+            by_class(functools.partial(send_corner_class, step), classes=ON_YZ)
         last = not fused
         stream_inside(step, 0, 1, last)
         lax.fori_loop(1, NX - 1, lambda x, _: stream_inside(step, x, 0, last), None, unroll=True)
         stream_inside(step, NX - 1, -1, last)
-
-        for sems, backward in ((send_sem, False), (recv_sem, True)):
-            by_class(
-                lambda dy, dz, sems=sems: await_bytes(
-                    sems, step + 1, CLASS[(dy, dz)], post_like(step, fused, dy, dz)
-                ),
-                backward,
-            )
-            for dx in (1, -1):
-                await_bytes(sems, step + 1, X_CLASS[dx], post_plane(step, dx, 0 if dx == 1 else NX + 1))
-                if fused:
-                    await_bytes(sems, step + 1, PART_CLASS[dx], post_part_got.at[step, SIDE[dx]])
+        await_posts(send_sem, step, CLASSES, False)
+        await_x(send_sem, step, fused)
         if fused:
-            finish_phase(step)
-        add_arrived(step, last)
+            await_corners(send_sem, step, False)
+        add_z, add_xy, add_across = arrivals(step, last)
+        await_posts(recv_sem, step, ON_Z, True)
+        add_z()
+        await_x(recv_sem, step, fused)
+        await_posts(recv_sem, step, ON_Y, True)
+        add_xy()
+        if fused:
+            finish_phase(step, True)
+        await_posts(recv_sem, step, ON_YZ, True)
+        add_across()
         lax.fori_loop(0, NX, lambda x, _: stream_across(step, x, last), None, unroll=True)
+        if fused:
+            lax.fori_loop(0, NX, lambda x, _: relax_body(step + 1, x, False), None, unroll=True)
+            await_corners(recv_sem, step, True)
+            finish_phase(step, False)
 
     def step_body(step, _):
         move(step, True)
-        lax.fori_loop(0, NX, lambda x, _: relax_body(step + 1, x, False), None, unroll=True)
 
     lax.fori_loop(0, STEPS - 1, step_body, None)
     move(STEPS - 1, False)
@@ -895,7 +943,7 @@
             vmem(2, 2, 1, NZ),
             vmem(STEPS, 2, ROWS_Y, 1, NZ),
             vmem(STEPS, 2, 8, NZ),
-            vmem(STEPS, 2, 2, 1, NZ),
+            vmem(STEPS, 2, 2, 1, 1, NZ),
             vmem(STEPS, 2, 2, ROWS_XY, 1, NZ),
             vmem(STEPS, 2, ROWS_PART, NZ),
             vmem(STEPS, 2, ROWS_Y_ALL, 1, NZ),
@@ -904,8 +952,8 @@
             vmem(STEPS, 2, ROWS_PART, NZ),
             vmem(2, *block),
             pltpu.SemaphoreType.DMA((3,)),
-            pltpu.SemaphoreType.DMA((1 + STEPS, 12)),
-            pltpu.SemaphoreType.DMA((1 + STEPS, 12)),
+            pltpu.SemaphoreType.DMA((1 + STEPS, 16)),
+            pltpu.SemaphoreType.DMA((1 + STEPS, 16)),
         ],
         compiler_params=pltpu.CompilerParams(
             collective_id=0, has_side_effects=True, vmem_limit_bytes=VMEM_LIMIT

time: 35.3 us -> 34.3 us (0.972)
  Pallas kernels: 34.6 us -> 33.5 us
    pallas_call x1, Pallas kernels: 33.6 us -> 32.5 us  [shards(): pl.pallas_call(functools.partial(kernel, sizes=sizes), out_shape=vmem(33,...]
where the time goes in v3:
time: 34.3 us; the launch traced here: 34.2 us
  Pallas kernels  33.5 us (98%)
  between operations  0.64 us (2%)
    pallas_call x1, Pallas kernels, shards(): pl.pallas_call(functools.partial(kernel, sizes=sizes), out_shape=vmem(33,...  32.5 us
    pallas_call x1, Pallas kernels, shards(): pl.pallas_call(hand_out, out_shape=[jax.ShapeDtypeStruct((count,) + block...  1 us

profile of v3, /device:TPU:1, one launch (start us, length us, event | category | flops | bytes accessed | tf_op | source)
XLA Modules:
  0.0 34.2 jit_solution(2278388746798275251)
XLA Ops:
  0.6 32.5 %shard_map.58.every = f32[33,4,16,128]{3,2,1,0:T(8,128)S(1)} custom-call(f32[19,4,16,128]{3,2,1,0:T(8,128)} %momentum_in.1, s32[4,16,128]{2,1,0:T(8,128)} %labels_in.1, s32[4,16,128]{2,1,0:T(8,128)} %solid_in.1), custom_call_target="tpu_custom_call" | custom-call | flops 15000000 | bytes 1800000 | tf_op jit(solution)/shard_map/pallas_call | solution.py:923
  33.2 1.0 %shard_map.59 = (f32[19,4,16,128]{3,2,1,0:T(8,128)}, f32[7,4,16,128]{3,2,1,0:T(8,128)}, f32[7,4,16,128]{3,2,1,0:T(8,128)}) custom-call(f32[33,4,16,128]{3,2,1,0:T(8,128)S(1)} %shard_map.58.every), custom_call_target="tpu_custom_call" | custom-call | bytes 2200000 | tf_op jit(solution)/shard_map/pallas_call | solution.py:963

commit v4 on v3

--- a/solution.py
+++ b/solution.py
@@ -65,10 +65,10 @@
 SUM_Y, X_Y, Z_Y, ROWS_Y = 28, 36, 40, 42
 Y_XY, SUM_XY, X_XY, ROWS_XY = 1, 3, 5, 7
 ROWS_Y_ALL = ROWS_Y + 2 * ROWS_XY
-Y_PART, Z_PART, ROWS_PART = 32, 40, 56
+Y_PART, Z_PART, ROWS_PART = 32, 40, 48
 ON_Y, ON_Z = ((1, 0), (-1, 0)), ((0, 1), (0, -1))
 ON_YZ = ((1, 1), (1, -1), (-1, 1), (-1, -1))
-CLASSES = ON_Y + ON_Z + ON_YZ
+CLASSES = ON_YZ + ON_Y + ON_Z
 CLASS = {way: place for place, way in enumerate(CLASSES)}
 X_CLASS = {1: 8, -1: 9}
 PART_CLASS = {1: 10, -1: 11}
@@ -200,14 +200,19 @@
     def post_plane(step, dx, plane):
         return posts.at[step, pl.ds(0 if dx == 1 else 7, 7), plane, pl.ds(LO, NY)]
 
-    def send_post_class(step, dy, dz):
+    def xy_place(dx, fused):
+        return ROWS_Y + ROWS_XY * SIDE[dx] if fused else SUM_Y + SIDE[dx]
+
+    def send_post_class(step, fused, dy, dz):
         turn, place = step + 1, CLASS[(dy, dz)]
         if dz == 0:
             side = SIDE[dy]
-            send(post_y.at[step, side], post_y_got.at[step, side, pl.ds(0, ROWS_Y)], turn, place, (0, dy, 0))
+            rows, rows_xy = pl.ds(0, ROWS_Y if fused else SUM_Y), ROWS_XY if fused else 1
+            send(post_y.at[step, side, rows], post_y_got.at[step, side, rows], turn, place, (0, dy, 0))
             for dx in (1, -1):
-                target = post_y_got.at[step, side, pl.ds(ROWS_Y + ROWS_XY * SIDE[dx], ROWS_XY)]
-                send(post_xy.at[step, SIDE[dx], side], target, turn, place, (dx, dy, 0))
+                source = post_xy.at[step, SIDE[dx], side, pl.ds(0, rows_xy)]
+                target = post_y_got.at[step, side, pl.ds(xy_place(dx, fused), rows_xy)]
+                send(source, target, turn, place, (dx, dy, 0))
         elif dy == 0:
             side = SIDE[dz]
             for dx in (0, 1, -1):
@@ -223,9 +228,9 @@
             target = post_row_got.at[step, sides[0], sides[1], pl.ds(TURN[dx], 1)]
             send(post_row.at[step, sides[0], sides[1]], target, step + 1, CORNER_CLASS[(dy, dz)], (dx, dy, dz))
 
-    def post_like(step, dy, dz):
+    def post_like(step, fused, dy, dz):
         if dz == 0:
-            return post_y_got.at[step, SIDE[dy]]
+            return post_y_got.at[step, SIDE[dy], pl.ds(0, ROWS_Y_ALL if fused else SUM_Y + 2)]
         if dy == 0:
             return post_z_got.at[step, SIDE[dz]]
         return post_row_got.at[step, SIDE[dy], SIDE[dz], pl.ds(0, 1)]
@@ -233,9 +238,11 @@
     def corner_like(step, dy, dz):
         return post_row_got.at[step, SIDE[dy], SIDE[dz], pl.ds(1, 2)]
 
-    def await_posts(sems, step, classes, backward):
+    def await_posts(sems, step, fused, classes, backward):
         by_class(
-            lambda dy, dz: await_bytes(sems, step + 1, CLASS[(dy, dz)], post_like(step, dy, dz)), backward, classes
+            lambda dy, dz: await_bytes(sems, step + 1, CLASS[(dy, dz)], post_like(step, fused, dy, dz)),
+            backward,
+            classes,
         )
 
     def await_corners(sems, step, backward):
@@ -245,11 +252,13 @@
             ON_YZ,
         )
 
-    def await_x(sems, step, fused):
+    def await_x(sems, step):
         for dx in (1, -1):
             await_bytes(sems, step + 1, X_CLASS[dx], post_plane(step, dx, 0 if dx == 1 else NX + 1))
-            if fused:
-                await_bytes(sems, step + 1, PART_CLASS[dx], post_part_got.at[step, SIDE[dx]])
+
+    def await_parts(sems, step):
+        for dx in (1, -1):
+            await_bytes(sems, step + 1, PART_CLASS[dx], post_part_got.at[step, SIDE[dx]])
 
     def pack_z(tile, place, sign, packed):
         moved = pltpu.roll(tile, place + 1 if sign == 1 else place, axis=1)
@@ -551,7 +560,7 @@
                             lane == edge_lane(dz), unpack_z(face, place, dz), posts[step, SLOT[name], x + 1, rows, :]
                         )
 
-        def add_xy():
+        def add_x():
             for dx, end, ghost, column, names in ((1, 0, 0, NX - 1, X_UP), (-1, NX - 1, NX + 1, 0, X_DOWN)):
                 for name in names:
                     if not wanted(name):
@@ -559,7 +568,7 @@
                     _, dy, dz = VELOCITY[name[1]]
                     if dy != 0:
                         row_ghost = LO - 1 if dy == 1 else HI
-                        line = post_y_got[step, SIDE[dy], ROWS_Y + ROWS_XY * SIDE[dx]]
+                        line = post_y_got[step, SIDE[dy], xy_place(dx, not last)]
                         posts[step, SLOT[name], ghost, row_ghost : row_ghost + 1, :] = line
                     for half in range(2):
                         rows = slice(8 * half, 8 * half + 8)
@@ -568,6 +577,7 @@
                         if dz != 0:
                             value = value + z_columns(name, dx, column, half)
                         state[state_at(name), end, rows, :] = state[state_at(name), end, rows, :] + kept(end, rows, value)
+        def add_y():
             for dy, edge in ((1, 0), (-1, NY - 1)):
                 rows = slice(edge, edge + 1)
                 for entry, name in enumerate(Y_FACE[dy]):
@@ -591,7 +601,7 @@
                     line = jnp.where(row_lane == edge_lane(dz), corner, post_y_got[step, SIDE[dy], entry * 4 + x])
                     posts[step, SLOT[name], x + 1, ghost : ghost + 1, :] = line
 
-        return add_z, add_xy, add_across
+        return add_x, add_y, add_z, add_across
 
     shifted_scalars = {0: scalars, 1: scalars_down, -1: scalars_up}
 
@@ -653,8 +663,8 @@
                 slot = SLOT[("f", VELOCITY.index((dx, dy, 0)))]
                 post_xy[step, SIDE[dx], SIDE[dy], 0] = posts[step, slot, end + 1, edge : edge + 1, :]
             if fused:
-                post_part[step, SIDE[dx], Z_PART : Z_PART + 8, :] = packed[0]
-                post_part[step, SIDE[dx], Z_PART + 8 : Z_PART + 16, :] = packed[1]
+                both = jnp.where(lane < 64, packed[0], pltpu.roll(packed[1], 64, axis=1))
+                post_part[step, SIDE[dx], Z_PART : Z_PART + 8, :] = both
         for dz in (1, -1):
             post_z[step, SIDE[dz]] = packed[SIDE[dz]]
             for dy, edge in ((1, 7), (-1, 0)):
@@ -673,7 +683,8 @@
         blue = turned(sums, 8)
         return ratio(sums, blue)
 
-    def finish_phase(step, inside):
+    def finish_phase(step, planes=(), corners=False):
+        inside = len(planes) > 0
         here_ = step + 2
 
         def put(target, entry, plane, rows, value):
@@ -684,7 +695,7 @@
         z_got = {(dx, dz): post_z_got[step, SIDE[dz], TURN[dx]] for dx in (-1, 0, 1) for dz in (1, -1)}
         row_got = {
             (dx, dy, dz): post_row_got[step, SIDE[dy], SIDE[dz], TURN[dx]]
-            for dx in (() if inside else (-1, 0, 1))
+            for dx in (() if inside else (-1, 0, 1) if corners else (0,))
             for dy in (1, -1)
             for dz in (1, -1)
         }
@@ -715,7 +726,7 @@
                 line = line + jnp.where(row_lane == edge_lane(dz), unpack_z(row_got[(dx, dy, dz)], lanes, dz), 0.0)
             return line
 
-        for x in range(NX) if inside else ():
+        for x in planes:
             sums = []
             for place, kind in enumerate(("r", "b")):
                 total = partial[place, x]
@@ -736,10 +747,12 @@
             sums = []
             lines = {1: [], -1: []}
             for place, kind in enumerate(("r", "b")):
-                total = post_part_got[step, SIDE[dx], NY * place : NY * place + NY, :]
-                total = total + posts[step, SLOT[(kind, FACE[(0, -dx)])], end + 1, interior, :]
-                rows = {dy: xy_got(dx, dy, Y_XY + place) for dy in (1, -1)}
-                sums.append(with_columns(with_rows(total, rows), place, column, dx))
+                if not corners:
+                    total = post_part_got[step, SIDE[dx], NY * place : NY * place + NY, :]
+                    total = total + posts[step, SLOT[(kind, FACE[(0, -dx)])], end + 1, interior, :]
+                    rows = {dy: xy_got(dx, dy, Y_XY + place) for dy in (1, -1)}
+                    sums.append(with_columns(with_rows(total, rows), place, column, dx))
+                    continue
                 for dy in (1, -1):
                     part = Y_PART + 2 * SIDE[-dy] + place
                     line = (
@@ -748,11 +761,13 @@
                         + post_y_got[step, SIDE[dy], X_Y + 2 * SIDE[-dx] + place]
                     )
                     lines[dy].append(with_ends(line, (dx, dy), place, column))
-            put(0, here_, ghost, interior, ratio(*sums))
+            if not corners:
+                put(0, here_, ghost, interior, ratio(*sums))
+                continue
             for dy, row_ghost in ((1, LO - 1), (-1, HI)):
                 put(0, here_, ghost, slice(row_ghost, row_ghost + 1), ratio(*lines[dy]))
         for dy, row_ghost, edge in ((1, LO - 1, LO), (-1, HI, HI - 1)):
-            for x in range(NX):
+            for x in () if corners else range(NX):
                 sums = []
                 for place, kind in enumerate(("r", "b")):
                     line = post_y_got[step, SIDE[dy], SUM_Y + 4 * place + x]
@@ -771,16 +786,17 @@
                 sums = sums + jnp.where(first_y, turned(row_got[(dx, 1, dz)], Y_Z), 0.0)
                 return sums + jnp.where(last_y, turned(row_got[(dx, -1, dz)], Y_Z), 0.0)
 
-            sums = turned(z_got[(0, dz)], SUM_Z) + turned(post_z[step, SIDE[-dz]], IN_Z)
-            sums = sums + jnp.where(low_x, turned(z_got[(1, dz)], X_Z), 0.0)
-            sums = sums + jnp.where(high_x, turned(z_got[(-1, dz)], X_Z), 0.0)
-            faces = {0: packed_ratio(with_y(sums, 0))}
-            for dx in (1, -1):
-                part = Z_PART + 8 * SIDE[-dz]
+            faces = {}
+            if not corners:
+                sums = turned(z_got[(0, dz)], SUM_Z) + turned(post_z[step, SIDE[-dz]], IN_Z)
+                sums = sums + jnp.where(low_x, turned(z_got[(1, dz)], X_Z), 0.0)
+                sums = sums + jnp.where(high_x, turned(z_got[(-1, dz)], X_Z), 0.0)
+                faces[0] = packed_ratio(with_y(sums, 0))
+            for dx in (1, -1) if corners else ():
                 sums = turned(z_got[(dx, dz)], SUM_Z) + turned(z_got[(0, dz)], X_Z)
-                sums = sums + turned(post_part_got[step, SIDE[dx], part : part + 8, :], IN_Z)
+                sums = sums + turned(post_part_got[step, SIDE[dx], Z_PART : Z_PART + 8, :], IN_Z + 64 * SIDE[-dz])
                 faces[dx] = packed_ratio(with_y(sums, dx))
-            for plane in range(NX + 2):
+            for plane in (0, NX + 1) if corners else range(1, NX + 1):
                 dx, column = {0: (1, NX - 1), NX + 1: (-1, 0)}.get(plane, (0, plane - 1))
                 for half in range(2):
                     rows = slice(LO + 8 * half, LO + 8 * half + 8)
@@ -794,10 +810,11 @@
                 sums = turned(row_got[(0, dy, dz)], SUM_Z)
                 sums = sums + turned(post_y_got[step, SIDE[dy], Z_Y + SIDE[-dz]], IN_Z)
                 sums = sums + turned(post_z_got[step, SIDE[dz], 0, edge : edge + 1, :], Y_Z)
-                sums = sums + jnp.where(row_low_x, turned(row_got[(1, dy, dz)], X_Z), 0.0)
-                sums = sums + jnp.where(row_high_x, turned(row_got[(-1, dy, dz)], X_Z), 0.0)
+                if corners:
+                    sums = sums + jnp.where(row_low_x, turned(row_got[(1, dy, dz)], X_Z), 0.0)
+                    sums = sums + jnp.where(row_high_x, turned(row_got[(-1, dy, dz)], X_Z), 0.0)
                 corner = packed_ratio(sums)
-                for x in range(NX):
+                for x in (0, NX - 1) if corners else range(1, NX - 1):
                     line = scalars[here_, x + 1, row_ghost : row_ghost + 1, :]
                     line = pltpu.roll(line, 1 if dz == 1 else 127, axis=1)
                     line = jnp.where(row_lane == edge_lane(dz), unpack_z(corner, 2 * x + half, dz), line)
@@ -813,7 +830,7 @@
     barrier = pltpu.get_barrier_semaphore()
 
     def greet(dy, dz):
-        for dx in (0, 1, -1):
+        for dx in (0, 1, -1) if 0 in (dy, dz) else (0,):
             pl.semaphore_signal(barrier, inc=1, device_id=neighbour((dx, dy, dz)), device_id_type=MESH)
 
     by_class(greet)
@@ -821,7 +838,7 @@
         pl.semaphore_signal(barrier, inc=1, device_id=neighbour((dx, 0, 0)), device_id_type=MESH)
     beside_y = 2 - closed[(1, 1)].astype(jnp.int32) - closed[(1, -1)].astype(jnp.int32)
     beside_z = 2 - closed[(2, 1)].astype(jnp.int32) - closed[(2, -1)].astype(jnp.int32)
-    beside = 2 + 3 * (beside_y + beside_z) + 3 * beside_y * beside_z
+    beside = 2 + 3 * (beside_y + beside_z) + beside_y * beside_z
 
     def clear(dy, dz):
         for step in range(STEPS):
@@ -838,10 +855,6 @@
     for step in range(STEPS):
         for side in range(2):
             post_part[step, side, Y_PART : Y_PART + 8, :] = blank
-            if step == STEPS - 1:
-                post_y[step, side, SUM_Y:ROWS_Y] = jnp.zeros((ROWS_Y - SUM_Y, 1, NZ), jnp.float32)
-                for other in range(2):
-                    post_xy[step, side, other, Y_XY:ROWS_XY] = jnp.zeros((ROWS_XY - Y_XY, 1, NZ), jnp.float32)
         for name in Y_FACE[1] + Y_FACE[-1]:
             if name not in ACROSS_YZ:
                 ghost = LO - 1 if VELOCITY[name[1]][1] == 1 else HI
@@ -857,50 +870,59 @@
     lax.fori_loop(0, NX, lambda x, _: relax_body(0, x, True), None, unroll=True)
     unpack_phase()
 
-    def move(step, fused):
-        packed = (blank, blank)
+    def collide_middle(step):
+        return lax.fori_loop(1, NX - 1, lambda x, p: collide_body(step, x, p), (blank, blank), unroll=True)
+
+    def move(step, packed, fused):
         packed = lax.fori_loop(0, 2, lambda turn, p: collide_body(step, 3 - 3 * turn, p), packed, unroll=True)
-        for dx, near, far in ((1, NX, 0), (-1, 1, NX + 1)):
-            send(post_plane(step, dx, near), post_plane(step, dx, far), step + 1, X_CLASS[dx], (dx, 0, 0))
-        packed = lax.fori_loop(1, 3, lambda x, p: collide_body(step, x, p), packed, unroll=True)
         if fused:
             packed = add_up(step, packed)
         put_edges(step, packed, fused)
-        by_class(functools.partial(send_post_class, step))
+        by_class(functools.partial(send_post_class, step, fused), classes=ON_Y + ON_YZ)
+        for dx, near, far in ((1, NX, 0), (-1, 1, NX + 1)):
+            send(post_plane(step, dx, near), post_plane(step, dx, far), step + 1, X_CLASS[dx], (dx, 0, 0))
+        if fused:
+            by_class(functools.partial(send_corner_class, step), classes=ON_YZ)
+        by_class(functools.partial(send_post_class, step, fused), classes=ON_Z)
         if fused:
             for dx in (1, -1):
                 side = SIDE[dx]
                 send(post_part.at[step, side], post_part_got.at[step, side], step + 1, PART_CLASS[dx], (dx, 0, 0))
-            by_class(functools.partial(send_corner_class, step), classes=ON_YZ)
         last = not fused
         stream_inside(step, 0, 1, last)
         lax.fori_loop(1, NX - 1, lambda x, _: stream_inside(step, x, 0, last), None, unroll=True)
         stream_inside(step, NX - 1, -1, last)
-        await_posts(send_sem, step, CLASSES, False)
-        await_x(send_sem, step, fused)
+        await_posts(send_sem, step, fused, CLASSES, False)
+        await_x(send_sem, step)
         if fused:
+            await_parts(send_sem, step)
             await_corners(send_sem, step, False)
-        add_z, add_xy, add_across = arrivals(step, last)
-        await_posts(recv_sem, step, ON_Z, True)
+        add_x, add_y, add_z, add_across = arrivals(step, last)
+        await_posts(recv_sem, step, fused, ON_Z, True)
         add_z()
-        await_x(recv_sem, step, fused)
-        await_posts(recv_sem, step, ON_Y, True)
-        add_xy()
+        await_posts(recv_sem, step, fused, ON_Y, True)
+        add_y()
         if fused:
-            finish_phase(step, True)
-        await_posts(recv_sem, step, ON_YZ, True)
+            finish_phase(step, (1, 2))
+        await_posts(recv_sem, step, fused, ON_YZ, True)
         add_across()
         lax.fori_loop(0, NX, lambda x, _: stream_across(step, x, last), None, unroll=True)
         if fused:
-            lax.fori_loop(0, NX, lambda x, _: relax_body(step + 1, x, False), None, unroll=True)
+            lax.fori_loop(1, 3, lambda x, _: relax_body(step + 1, x, False), None, unroll=True)
+        await_x(recv_sem, step)
+        add_x()
+        if fused:
+            finish_phase(step, (0, 3))
+            lax.fori_loop(0, 2, lambda turn, _: relax_body(step + 1, 3 - 3 * turn, False), None, unroll=True)
+            await_parts(recv_sem, step)
+            finish_phase(step)
+            packed = collide_middle(step + 1)
             await_corners(recv_sem, step, True)
-            finish_phase(step, False)
-
-    def step_body(step, _):
-        move(step, True)
-
-    lax.fori_loop(0, STEPS - 1, step_body, None)
-    move(STEPS - 1, False)
+            finish_phase(step, corners=True)
+        return packed
+
+    packed = lax.fori_loop(0, STEPS - 1, lambda step, p: move(step, p, True), collide_middle(0))
+    move(STEPS - 1, packed, False)
 
 
 def hand_out(every, momentum_out, red_out, blue_out, sem):

time: 34.3 us -> 33.4 us (0.974)
  Pallas kernels: 33.5 us -> 32.7 us
    pallas_call x1, Pallas kernels: 32.5 us -> 31.7 us  [shards(): pl.pallas_call(functools.partial(kernel, sizes=sizes), out_shape=vmem(33,...]
where the time goes in v4:
time: 33.4 us; the launch traced here: 33.3 us
  Pallas kernels  32.7 us (98%)
  between operations  0.64 us (2%)
    pallas_call x1, Pallas kernels, shards(): pl.pallas_call(functools.partial(kernel, sizes=sizes), out_shape=vmem(33,...  31.7 us
    pallas_call x1, Pallas kernels, shards(): pl.pallas_call(hand_out, out_shape=[jax.ShapeDtypeStruct((count,) + block...  1 us

profile of v4, /device:TPU:1, one launch (start us, length us, event | category | flops | bytes accessed | tf_op | source)
XLA Modules:
  0.0 33.3 jit_solution(8811714348755541147)
XLA Ops:
  0.6 31.7 %shard_map.58.every = f32[33,4,16,128]{3,2,1,0:T(8,128)S(1)} custom-call(f32[19,4,16,128]{3,2,1,0:T(8,128)} %momentum_in.1, s32[4,16,128]{2,1,0:T(8,128)} %labels_in.1, s32[4,16,128]{2,1,0:T(8,128)} %solid_in.1), custom_call_target="tpu_custom_call" | custom-call | flops 15000000 | bytes 1800000 | tf_op jit(solution)/shard_map/pallas_call | solution.py:945
  32.3 1.0 %shard_map.59 = (f32[19,4,16,128]{3,2,1,0:T(8,128)}, f32[7,4,16,128]{3,2,1,0:T(8,128)}, f32[7,4,16,128]{3,2,1,0:T(8,128)}) custom-call(f32[33,4,16,128]{3,2,1,0:T(8,128)S(1)} %shard_map.58.every), custom_call_target="tpu_custom_call" | custom-call | bytes 2200000 | tf_op jit(solution)/shard_map/pallas_call | solution.py:985

commit v5 on v4

--- a/solution.py
+++ b/solution.py
@@ -106,6 +106,8 @@
     post_row_got,
     post_part_got,
     partial,
+    zero_rows,
+    zero_tiles,
     in_sem,
     send_sem,
     recv_sem,
@@ -140,9 +142,9 @@
         else:
             pl.when(condition)(action)
 
-    def by_class(action, backward=False, classes=CLASSES):
+    def by_class(action, always=False, classes=CLASSES):
         for dy, dz in classes:
-            when(has((0, -dy, -dz) if backward else (0, dy, dz)), functools.partial(action, dy, dz))
+            when(None if always else has((0, dy, dz)), functools.partial(action, dy, dz))
 
     lane = lax.broadcasted_iota(jnp.int32, (8, NZ), 1)
     wide_lane = lax.broadcasted_iota(jnp.int32, (NY, NZ), 1)
@@ -287,7 +289,7 @@
         for dz in (1, -1):
             phase_z[SIDE[dz]] = packed[SIDE[dz]]
             for dy, edge in ((1, 7), (-1, 0)):
-                phase_yz[SIDE[dy], SIDE[dz]] = phase_z[SIDE[dz], edge : edge + 1, :]
+                phase_yz[SIDE[dy], SIDE[dz], 0] = phase_z[SIDE[dz], edge : edge + 1, :]
         by_class(send_phase_class)
         for dx, near, far in ((1, NX, 0), (-1, 1, NX + 1)):
             send(phase_plane(near), phase_plane(far), 0, X_CLASS[dx], (dx, 0, 0))
@@ -335,7 +337,7 @@
                     line = cover((0, dy, 0), phase_y_got[SIDE[dy], x * count + entry], fills[entry])
                     scalars[first + entry, x + 1, ghost : ghost + 1, :] = line
                     for dz in (1, -1):
-                        corner = phase_yz_got[SIDE[dy], SIDE[dz]]
+                        corner = phase_yz_got[SIDE[dy], SIDE[dz], 0]
                         place = entry * 8 + 2 * x + half
                         corner = cover((0, dy, dz), unpack_z(corner, place, dz), fills[entry])
                         shifted[dz][place_of(entry), x + 1, ghost : ghost + 1, :] = jnp.where(
@@ -840,14 +842,20 @@
     beside_z = 2 - closed[(2, 1)].astype(jnp.int32) - closed[(2, -1)].astype(jnp.int32)
     beside = 2 + 3 * (beside_y + beside_z) + beside_y * beside_z
 
+    zero_rows[...] = jnp.zeros((ROWS_Y_ALL, 1, NZ), jnp.float32)
+    zero_tiles[...] = jnp.zeros((3, 8, NZ), jnp.float32)
+
     def clear(dy, dz):
+        def fill(target, turn, place):
+            source = zero_tiles if dy == 0 else zero_rows.at[pl.ds(0, target.shape[0])]
+            pltpu.make_async_copy(source, target, recv_sem.at[turn, place]).start()
+
+        fill(phase_like(dy, dz), 0, CLASS[(dy, dz)])
         for step in range(STEPS):
-            if dz == 0:
-                post_y_got[step, SIDE[dy]] = jnp.zeros((ROWS_Y_ALL, 1, NZ), jnp.float32)
-            elif dy == 0:
-                post_z_got[step, SIDE[dz]] = jnp.zeros((3, 8, NZ), jnp.float32)
-            else:
-                post_row_got[step, SIDE[dy], SIDE[dz]] = jnp.zeros((3, 1, NZ), jnp.float32)
+            fused = step < STEPS - 1
+            fill(post_like(step, fused, dy, dz), step + 1, CLASS[(dy, dz)])
+            if fused and dy != 0 and dz != 0:
+                fill(corner_like(step, dy, dz), step + 1, CORNER_CLASS[(dy, dz)])
 
     for dy, dz in CLASSES:
         pl.when(jnp.logical_not(has((0, -dy, -dz))))(functools.partial(clear, dy, dz))
@@ -959,10 +967,10 @@
             vmem(2, *block),
             vmem(2, 8, 1, NZ),
             vmem(2, 8, NZ),
-            vmem(2, 2, 1, NZ),
+            vmem(2, 2, 1, 1, NZ),
             vmem(2, 12, 1, NZ),
             vmem(2, 3, 8, NZ),
-            vmem(2, 2, 1, NZ),
+            vmem(2, 2, 1, 1, NZ),
             vmem(STEPS, 2, ROWS_Y, 1, NZ),
             vmem(STEPS, 2, 8, NZ),
             vmem(STEPS, 2, 2, 1, 1, NZ),
@@ -973,6 +981,8 @@
             vmem(STEPS, 2, 2, 3, 1, NZ),
             vmem(STEPS, 2, ROWS_PART, NZ),
             vmem(2, *block),
+            vmem(ROWS_Y_ALL, 1, NZ),
+            vmem(3, 8, NZ),
             pltpu.SemaphoreType.DMA((3,)),
             pltpu.SemaphoreType.DMA((1 + STEPS, 16)),
             pltpu.SemaphoreType.DMA((1 + STEPS, 16)),

time: 33.4 us -> 33.4 us (level)
  no operation moved by 1% of the time
where the time goes in v5:
time: 33.4 us; the launch traced here: 33.3 us
  Pallas kernels  32.7 us (98%)
  between operations  0.64 us (2%)
    pallas_call x1, Pallas kernels, shards(): pl.pallas_call(functools.partial(kernel, sizes=sizes), out_shape=vmem(33,...  31.7 us
    pallas_call x1, Pallas kernels, shards(): pl.pallas_call(hand_out, out_shape=[jax.ShapeDtypeStruct((count,) + block...  1 us

profile of v5, /device:TPU:1, one launch (start us, length us, event | category | flops | bytes accessed | tf_op | source)
XLA Modules:
  0.0 33.3 jit_solution(9925285617310281116)
XLA Ops:
  0.6 31.7 %shard_map.58.every = f32[33,4,16,128]{3,2,1,0:T(8,128)S(1)} custom-call(f32[19,4,16,128]{3,2,1,0:T(8,128)} %momentum_in.1, s32[4,16,128]{2,1,0:T(8,128)} %labels_in.1, s32[4,16,128]{2,1,0:T(8,128)} %solid_in.1), custom_call_target="tpu_custom_call" | custom-call | flops 15000000 | bytes 1800000 | tf_op jit(solution)/shard_map/pallas_call | solution.py:953
  32.3 1.0 %shard_map.59 = (f32[19,4,16,128]{3,2,1,0:T(8,128)}, f32[7,4,16,128]{3,2,1,0:T(8,128)}, f32[7,4,16,128]{3,2,1,0:T(8,128)}) custom-call(f32[33,4,16,128]{3,2,1,0:T(8,128)S(1)} %shard_map.58.every), custom_call_target="tpu_custom_call" | custom-call | bytes 2200000 | tf_op jit(solution)/shard_map/pallas_call | solution.py:995

commit v6 on v4

--- a/solution.py
+++ b/solution.py
@@ -879,10 +879,10 @@
             packed = add_up(step, packed)
         put_edges(step, packed, fused)
         by_class(functools.partial(send_post_class, step, fused), classes=ON_Y + ON_YZ)
+        if fused:
+            by_class(functools.partial(send_corner_class, step), classes=ON_YZ)
         for dx, near, far in ((1, NX, 0), (-1, 1, NX + 1)):
             send(post_plane(step, dx, near), post_plane(step, dx, far), step + 1, X_CLASS[dx], (dx, 0, 0))
-        if fused:
-            by_class(functools.partial(send_corner_class, step), classes=ON_YZ)
         by_class(functools.partial(send_post_class, step, fused), classes=ON_Z)
         if fused:
             for dx in (1, -1):

time: 33.4 us -> 33.4 us (level)
  no operation moved by 1% of the time
where the time goes in v6:
time: 33.4 us; the launch traced here: 33.3 us
  Pallas kernels  32.7 us (98%)
  between operations  0.64 us (2%)
    pallas_call x1, Pallas kernels, shards(): pl.pallas_call(functools.partial(kernel, sizes=sizes), out_shape=vmem(33,...  31.7 us
    pallas_call x1, Pallas kernels, shards(): pl.pallas_call(hand_out, out_shape=[jax.ShapeDtypeStruct((count,) + block...  1 us

profile of v6, /device:TPU:1, one launch (start us, length us, event | category | flops | bytes accessed | tf_op | source)
XLA Modules:
  0.0 33.3 jit_solution(8742564863935985857)
XLA Ops:
  0.6 31.7 %shard_map.58.every = f32[33,4,16,128]{3,2,1,0:T(8,128)S(1)} custom-call(f32[19,4,16,128]{3,2,1,0:T(8,128)} %momentum_in.1, s32[4,16,128]{2,1,0:T(8,128)} %labels_in.1, s32[4,16,128]{2,1,0:T(8,128)} %solid_in.1), custom_call_target="tpu_custom_call" | custom-call | flops 15000000 | bytes 1800000 | tf_op jit(solution)/shard_map/pallas_call | solution.py:945
  32.3 1.0 %shard_map.59 = (f32[19,4,16,128]{3,2,1,0:T(8,128)}, f32[7,4,16,128]{3,2,1,0:T(8,128)}, f32[7,4,16,128]{3,2,1,0:T(8,128)}) custom-call(f32[33,4,16,128]{3,2,1,0:T(8,128)S(1)} %shard_map.58.every), custom_call_target="tpu_custom_call" | custom-call | bytes 2200000 | tf_op jit(solution)/shard_map/pallas_call | solution.py:985

commit v7 on v6

--- a/solution.py
+++ b/solution.py
@@ -62,9 +62,10 @@
 TURN = {0: 0, 1: 1, -1: 2}
 FACE = {(1, 1): 3, (1, -1): 4, (0, 1): 1, (0, -1): 2, (2, 1): 5, (2, -1): 6}
 IN_Z, SUM_Z, X_Z, Y_Z = 40, 56, 72, 88
-SUM_Y, X_Y, Z_Y, ROWS_Y = 28, 36, 40, 42
-Y_XY, SUM_XY, X_XY, ROWS_XY = 1, 3, 5, 7
+SUM_Y, X_Y, Z_Y, ROWS_Y = 28, 36, 40, 48
+Y_XY, SUM_XY, X_XY, ROWS_XY = 1, 3, 5, 8
 ROWS_Y_ALL = ROWS_Y + 2 * ROWS_XY
+ROWS_Y_LAST = 32
 Y_PART, Z_PART, ROWS_PART = 32, 40, 48
 ON_Y, ON_Z = ((1, 0), (-1, 0)), ((0, 1), (0, -1))
 ON_YZ = ((1, 1), (1, -1), (-1, 1), (-1, -1))
@@ -201,17 +202,17 @@
         return posts.at[step, pl.ds(0 if dx == 1 else 7, 7), plane, pl.ds(LO, NY)]
 
     def xy_place(dx, fused):
-        return ROWS_Y + ROWS_XY * SIDE[dx] if fused else SUM_Y + SIDE[dx]
+        return (ROWS_Y if fused else ROWS_Y_LAST) + ROWS_XY * SIDE[dx]
 
     def send_post_class(step, fused, dy, dz):
         turn, place = step + 1, CLASS[(dy, dz)]
         if dz == 0:
             side = SIDE[dy]
-            rows, rows_xy = pl.ds(0, ROWS_Y if fused else SUM_Y), ROWS_XY if fused else 1
+            rows = pl.ds(0, ROWS_Y if fused else ROWS_Y_LAST)
             send(post_y.at[step, side, rows], post_y_got.at[step, side, rows], turn, place, (0, dy, 0))
             for dx in (1, -1):
-                source = post_xy.at[step, SIDE[dx], side, pl.ds(0, rows_xy)]
-                target = post_y_got.at[step, side, pl.ds(xy_place(dx, fused), rows_xy)]
+                source = post_xy.at[step, SIDE[dx], side]
+                target = post_y_got.at[step, side, pl.ds(xy_place(dx, fused), ROWS_XY)]
                 send(source, target, turn, place, (dx, dy, 0))
         elif dy == 0:
             side = SIDE[dz]
@@ -230,7 +231,7 @@
 
     def post_like(step, fused, dy, dz):
         if dz == 0:
-            return post_y_got.at[step, SIDE[dy], pl.ds(0, ROWS_Y_ALL if fused else SUM_Y + 2)]
+            return post_y_got.at[step, SIDE[dy], pl.ds(0, (ROWS_Y if fused else ROWS_Y_LAST) + 2 * ROWS_XY)]
         if dy == 0:
             return post_z_got.at[step, SIDE[dz]]
         return post_row_got.at[step, SIDE[dy], SIDE[dz], pl.ds(0, 1)]
@@ -448,7 +449,7 @@
         posts[step, SLOT[name], x + 1, LO:HI, :] = value
         if offset[1] != 0:
             line = Y_FACE[sign].index(name) * 4 + x
-            post_y[step, SIDE[sign], line] = posts[step, SLOT[name], x + 1, edge : edge + 1, :]
+            post_y[step, SIDE[sign], pl.ds(line, 1), :] = posts[step, SLOT[name], x + 1, edge : edge + 1, :]
         return up, down
 
     def collide_body(step, x, packed):
@@ -568,7 +569,7 @@
                     _, dy, dz = VELOCITY[name[1]]
                     if dy != 0:
                         row_ghost = LO - 1 if dy == 1 else HI
-                        line = post_y_got[step, SIDE[dy], xy_place(dx, not last)]
+                        line = post_y_got[step, SIDE[dy], pl.ds(xy_place(dx, not last), 1), :]
                         posts[step, SLOT[name], ghost, row_ghost : row_ghost + 1, :] = line
                     for half in range(2):
                         rows = slice(8 * half, 8 * half + 8)
@@ -587,7 +588,7 @@
                         source = x - VELOCITY[name[1]][0]
                         if not 0 <= source < NX:
                             continue
-                        value = kept(x, rows, post_y_got[step, SIDE[dy], entry * 4 + source])
+                        value = kept(x, rows, post_y_got[step, SIDE[dy], pl.ds(entry * 4 + source, 1), :])
                         state[state_at(name), x, rows, :] = state[state_at(name), x, rows, :] + value
 
         def add_across():
@@ -598,7 +599,7 @@
                 ghost = LO - 1 if dy == 1 else HI
                 for x in range(NX):
                     corner = unpack_z(post_row_got[step, SIDE[dy], SIDE[dz], 0], entry_z * 8 + 2 * x + half, dz)
-                    line = jnp.where(row_lane == edge_lane(dz), corner, post_y_got[step, SIDE[dy], entry * 4 + x])
+                    line = jnp.where(row_lane == edge_lane(dz), corner, post_y_got[step, SIDE[dy], pl.ds(entry * 4 + x, 1), :])
                     posts[step, SLOT[name], x + 1, ghost : ghost + 1, :] = line
 
         return add_x, add_y, add_z, add_across
@@ -633,7 +634,7 @@
                     if x == end:
                         post_part[step, SIDE[dx], NY * place : NY * place + NY, :] = total
                 for dy, edge in ((1, NY - 1), (-1, 0)):
-                    post_y[step, SIDE[dy], SUM_Y + 4 * place + x] = partial[place, x, edge : edge + 1, :]
+                    post_y[step, SIDE[dy], pl.ds(SUM_Y + 4 * place + x, 1), :] = partial[place, x, edge : edge + 1, :]
                 for dy, half in ((1, 1), (-1, 0)):
                     rows = slice(LO + 8 * half, LO + 8 * half + 8)
                     tile = posts[step, SLOT[(kind, FACE[(1, dy)])], x + 1, rows, :]
@@ -648,11 +649,11 @@
                     up, down = pack_z(tile, lanes, 1, up), pack_z(tile, lanes, -1, down)
                 for dy, edge in ((1, HI - 1), (-1, LO)):
                     line = posts[step, slot, end + 1, edge : edge + 1, :]
-                    post_y[step, SIDE[dy], X_Y + 2 * SIDE[dx] + place] = line
-                    post_xy[step, SIDE[dx], SIDE[dy], X_XY + place] = line
-                    post_xy[step, SIDE[dx], SIDE[dy], SUM_XY + place] = partial[place, end, edge - LO : edge - LO + 1, :]
+                    post_y[step, SIDE[dy], pl.ds(X_Y + 2 * SIDE[dx] + place, 1), :] = line
+                    post_xy[step, SIDE[dx], SIDE[dy], pl.ds(X_XY + place, 1), :] = line
+                    post_xy[step, SIDE[dx], SIDE[dy], pl.ds(SUM_XY + place, 1), :] = partial[place, end, edge - LO : edge - LO + 1, :]
                     line = posts[step, SLOT[(kind, FACE[(1, dy)])], end + 1, edge : edge + 1, :]
-                    post_xy[step, SIDE[dx], SIDE[dy], Y_XY + place] = line
+                    post_xy[step, SIDE[dx], SIDE[dy], pl.ds(Y_XY + place, 1), :] = line
                     part = Y_PART + 2 * SIDE[dy] + place
                     post_part[step, SIDE[dx], part : part + 1, :] = line
         return up, down
@@ -661,7 +662,7 @@
         for dx, end in ((1, NX - 1), (-1, 0)):
             for dy, edge in ((1, HI - 1), (-1, LO)):
                 slot = SLOT[("f", VELOCITY.index((dx, dy, 0)))]
-                post_xy[step, SIDE[dx], SIDE[dy], 0] = posts[step, slot, end + 1, edge : edge + 1, :]
+                post_xy[step, SIDE[dx], SIDE[dy], pl.ds(0, 1), :] = posts[step, slot, end + 1, edge : edge + 1, :]
             if fused:
                 both = jnp.where(lane < 64, packed[0], pltpu.roll(packed[1], 64, axis=1))
                 post_part[step, SIDE[dx], Z_PART : Z_PART + 8, :] = both
@@ -671,7 +672,7 @@
                 line = post_z[step, SIDE[dz], edge : edge + 1, :]
                 post_row[step, SIDE[dy], SIDE[dz], 0] = line
                 if fused:
-                    post_y[step, SIDE[dy], Z_Y + SIDE[dz]] = line
+                    post_y[step, SIDE[dy], pl.ds(Z_Y + SIDE[dz], 1), :] = line
 
     def turned(value, lanes):
         return pltpu.roll(value, 128 - lanes, axis=1)
@@ -701,7 +702,7 @@
         }
 
         def xy_got(dx, dy, line):
-            return post_y_got[step, SIDE[dy], ROWS_Y + ROWS_XY * SIDE[dx] + line]
+            return post_y_got[step, SIDE[dy], pl.ds(ROWS_Y + ROWS_XY * SIDE[dx] + line, 1), :]
 
         def with_columns(value, place, column, dx):
             halves = []
@@ -736,7 +737,7 @@
                 rows = {}
                 for dy in (1, -1):
                     entry = Y_FACE[dy].index((kind, FACE[(1, dy)]))
-                    rows[dy] = post_y_got[step, SIDE[dy], entry * 4 + x]
+                    rows[dy] = post_y_got[step, SIDE[dy], pl.ds(entry * 4 + x, 1), :]
                 total = with_columns(with_rows(total, rows), place, x, 0)
                 colour[place, x] = total
                 sums.append(total)
@@ -758,7 +759,7 @@
                     line = (
                         xy_got(dx, dy, SUM_XY + place)
                         + post_part_got[step, SIDE[dx], part : part + 1, :]
-                        + post_y_got[step, SIDE[dy], X_Y + 2 * SIDE[-dx] + place]
+                        + post_y_got[step, SIDE[dy], pl.ds(X_Y + 2 * SIDE[-dx] + place, 1), :]
                     )
                     lines[dy].append(with_ends(line, (dx, dy), place, column))
             if not corners:
@@ -770,7 +771,7 @@
             for x in () if corners else range(NX):
                 sums = []
                 for place, kind in enumerate(("r", "b")):
-                    line = post_y_got[step, SIDE[dy], SUM_Y + 4 * place + x]
+                    line = post_y_got[step, SIDE[dy], pl.ds(SUM_Y + 4 * place + x, 1), :]
                     line = line + posts[step, SLOT[(kind, FACE[(1, -dy)])], x + 1, edge : edge + 1, :]
                     for dx, end in ((1, 0), (-1, NX - 1)):
                         if x == end:
@@ -808,7 +809,7 @@
                 half = 1 if dy == 1 else 0
                 edge = 0 if dy == 1 else 7
                 sums = turned(row_got[(0, dy, dz)], SUM_Z)
-                sums = sums + turned(post_y_got[step, SIDE[dy], Z_Y + SIDE[-dz]], IN_Z)
+                sums = sums + turned(post_y_got[step, SIDE[dy], pl.ds(Z_Y + SIDE[-dz], 1), :], IN_Z)
                 sums = sums + turned(post_z_got[step, SIDE[dz], 0, edge : edge + 1, :], Y_Z)
                 if corners:
                     sums = sums + jnp.where(row_low_x, turned(row_got[(1, dy, dz)], X_Z), 0.0)
@@ -843,7 +844,7 @@
     def clear(dy, dz):
         for step in range(STEPS):
             if dz == 0:
-                post_y_got[step, SIDE[dy]] = jnp.zeros((ROWS_Y_ALL, 1, NZ), jnp.float32)
+                post_y_got[step, SIDE[dy]] = jnp.zeros((ROWS_Y_ALL, NZ), jnp.float32)
             elif dy == 0:
                 post_z_got[step, SIDE[dz]] = jnp.zeros((3, 8, NZ), jnp.float32)
             else:
@@ -963,12 +964,12 @@
             vmem(2, 12, 1, NZ),
             vmem(2, 3, 8, NZ),
             vmem(2, 2, 1, NZ),
-            vmem(STEPS, 2, ROWS_Y, 1, NZ),
+            vmem(STEPS, 2, ROWS_Y, NZ),
             vmem(STEPS, 2, 8, NZ),
             vmem(STEPS, 2, 2, 1, 1, NZ),
-            vmem(STEPS, 2, 2, ROWS_XY, 1, NZ),
+            vmem(STEPS, 2, 2, ROWS_XY, NZ),
             vmem(STEPS, 2, ROWS_PART, NZ),
-            vmem(STEPS, 2, ROWS_Y_ALL, 1, NZ),
+            vmem(STEPS, 2, ROWS_Y_ALL, NZ),
             vmem(STEPS, 2, 3, 8, NZ),
             vmem(STEPS, 2, 2, 3, 1, NZ),
             vmem(STEPS, 2, ROWS_PART, NZ),

time: 33.4 us -> 33.4 us (level)
  no operation moved by 1% of the time
where the time goes in v7:
time: 33.4 us
  Pallas kernels  32.7 us (98%)
  between operations  0.64 us (2%)
    pallas_call x1, Pallas kernels, shards(): pl.pallas_call(functools.partial(kernel, sizes=sizes), out_shape=vmem(33,...  31.7 us
    pallas_call x1, Pallas kernels, shards(): pl.pallas_call(hand_out, out_shape=[jax.ShapeDtypeStruct((count,) + block...  1 us

profile of v7, /device:TPU:1, one launch (start us, length us, event | category | flops | bytes accessed | tf_op | source)
XLA Modules:
  0.0 33.4 jit_solution(11703022846097164459)
XLA Ops:
  0.6 31.7 %shard_map.58.every = f32[33,4,16,128]{3,2,1,0:T(8,128)S(1)} custom-call(f32[19,4,16,128]{3,2,1,0:T(8,128)} %momentum_in.1, s32[4,16,128]{2,1,0:T(8,128)} %labels_in.1, s32[4,16,128]{2,1,0:T(8,128)} %solid_in.1), custom_call_target="tpu_custom_call" | custom-call | flops 15000000 | bytes 1800000 | tf_op jit(solution)/shard_map/pallas_call | solution.py:946
  32.4 1.0 %shard_map.59 = (f32[19,4,16,128]{3,2,1,0:T(8,128)}, f32[7,4,16,128]{3,2,1,0:T(8,128)}, f32[7,4,16,128]{3,2,1,0:T(8,128)}) custom-call(f32[33,4,16,128]{3,2,1,0:T(8,128)S(1)} %shard_map.58.every), custom_call_target="tpu_custom_call" | custom-call | bytes 2200000 | tf_op jit(solution)/shard_map/pallas_call | solution.py:986

commit v8 on v6

--- a/solution.py
+++ b/solution.py
@@ -863,11 +863,11 @@
 
     loads[0].wait()
     loads[1].wait()
-    packed = lax.fori_loop(0, NX, first_phase, (blank, blank), unroll=True)
+    packed = lax.fori_loop(0, NX, first_phase, (blank, blank), unroll=False)
     pl.semaphore_wait(barrier, beside)
     send_phase(packed)
     loads[2].wait()
-    lax.fori_loop(0, NX, lambda x, _: relax_body(0, x, True), None, unroll=True)
+    lax.fori_loop(0, NX, lambda x, _: relax_body(0, x, True), None, unroll=False)
     unpack_phase()
 
     def collide_middle(step):
@@ -890,7 +890,7 @@
                 send(post_part.at[step, side], post_part_got.at[step, side], step + 1, PART_CLASS[dx], (dx, 0, 0))
         last = not fused
         stream_inside(step, 0, 1, last)
-        lax.fori_loop(1, NX - 1, lambda x, _: stream_inside(step, x, 0, last), None, unroll=True)
+        lax.fori_loop(1, NX - 1, lambda x, _: stream_inside(step, x, 0, last), None, unroll=False)
         stream_inside(step, NX - 1, -1, last)
         await_posts(send_sem, step, fused, CLASSES, False)
         await_x(send_sem, step)
@@ -906,14 +906,14 @@
             finish_phase(step, (1, 2))
         await_posts(recv_sem, step, fused, ON_YZ, True)
         add_across()
-        lax.fori_loop(0, NX, lambda x, _: stream_across(step, x, last), None, unroll=True)
+        lax.fori_loop(0, NX, lambda x, _: stream_across(step, x, last), None, unroll=False)
         if fused:
-            lax.fori_loop(1, 3, lambda x, _: relax_body(step + 1, x, False), None, unroll=True)
+            lax.fori_loop(1, 3, lambda x, _: relax_body(step + 1, x, False), None, unroll=False)
         await_x(recv_sem, step)
         add_x()
         if fused:
             finish_phase(step, (0, 3))
-            lax.fori_loop(0, 2, lambda turn, _: relax_body(step + 1, 3 - 3 * turn, False), None, unroll=True)
+            lax.fori_loop(0, 2, lambda turn, _: relax_body(step + 1, 3 - 3 * turn, False), None, unroll=False)
             await_parts(recv_sem, step)
             finish_phase(step)
             packed = collide_middle(step + 1)

time: 33.4 us -> 33.6 us (level)
  no operation moved by 1% of the time
where the time goes in v8:
time: 33.6 us; the launch traced here: 33.5 us
  Pallas kernels  32.9 us (98%)
  between operations  0.64 us (2%)
    pallas_call x1, Pallas kernels, shards(): pl.pallas_call(functools.partial(kernel, sizes=sizes), out_shape=vmem(33,...  31.9 us
    pallas_call x1, Pallas kernels, shards(): pl.pallas_call(hand_out, out_shape=[jax.ShapeDtypeStruct((count,) + block...  1 us

profile of v8, /device:TPU:1, one launch (start us, length us, event | category | flops | bytes accessed | tf_op | source)
XLA Modules:
  0.0 33.5 jit_solution(2753757177487460768)
XLA Ops:
  0.6 31.9 %shard_map.58.every = f32[33,4,16,128]{3,2,1,0:T(8,128)S(1)} custom-call(f32[19,4,16,128]{3,2,1,0:T(8,128)} %momentum_in.1, s32[4,16,128]{2,1,0:T(8,128)} %labels_in.1, s32[4,16,128]{2,1,0:T(8,128)} %solid_in.1), custom_call_target="tpu_custom_call" | custom-call | flops 15000000 | bytes 1800000 | tf_op jit(solution)/shard_map/pallas_call | solution.py:945
  32.5 1.0 %shard_map.59 = (f32[19,4,16,128]{3,2,1,0:T(8,128)}, f32[7,4,16,128]{3,2,1,0:T(8,128)}, f32[7,4,16,128]{3,2,1,0:T(8,128)}) custom-call(f32[33,4,16,128]{3,2,1,0:T(8,128)S(1)} %shard_map.58.every), custom_call_target="tpu_custom_call" | custom-call | bytes 2200000 | tf_op jit(solution)/shard_map/pallas_call | solution.py:985
